TPU v7x, 128 devices: a whole 4x4x4 slice. The times are simulated.
128 devices in a mesh: gy: 16 (over y_lo, x, core), gx: 8 (over z, y_hi).
Axes of the slice: x: 4, y: 4 (y_hi: 2, y_lo: 2; y = y_hi * 2 + y_lo), z: 4, core: 2. Of those that a mesh axis runs over, the one named last changes fastest.
Arguments:
- tokens: bfloat16 [8, 128, 256, 192], P(None, 'gy', 'gx'), may hold values from -6 to 6
- cotangent: bfloat16 [8, 128, 256, 192], P(None, 'gy', 'gx'), may hold values from -3 to 3
- gains: float32 [2, 192], replicated, may hold values from 0.1 to 1.9
- qkv_weight: bfloat16 [2, 192, 576], replicated, may hold values from -1.4433757 to 1.4433757, as said below
- proj_weight: bfloat16 [2, 192, 192], replicated, may hold values from -0.4375 to 0.4375
Outputs:
- grad_tokens: float32 [8, 128, 256, 192], P(None, 'gy', 'gx')
- grad_gains: float32 [2, 192], replicated
- grad_qkv: float32 [2, 192, 576], replicated
- grad_proj: float32 [2, 192, 192], replicated
Inputs may be any that keep to these rules, and one draw needn't show every extreme that they name: `qkv_weight`: the last dimension holds the query, key and value projections in that order.
All inputs are finite; a program needn't handle non-finite values.
Results may differ from a plain program's by a relative error of at most 0.02.
The roundings to bfloat16 on the way count: a program that leaves them out, or rounds other values in their place, can miss the bound.
Values may be sent and summed in bfloat16 or wider, within the bound.
A program may use at most 128 MiB of HBM per device.

v0:
```python
import jax
import jax.numpy as jnp
from jax import lax
from jax.sharding import PartitionSpec as P

HEADS = 6
WIN = 8


EPSILON = 1e-05
MASKED = -1e30


def passed_along(value, axis, steps):
    count = lax.axis_size(axis)
    pairs = [(source, (source + steps) % count) for source in range(count)]
    return lax.ppermute(value, axis, pairs)


def windows_of(cells, window_size):
    depth_count, row_count, col_count, features = cells.shape
    blocks = cells.reshape(
        depth_count // window_size,
        window_size,
        row_count // window_size,
        window_size,
        col_count // window_size,
        window_size,
        features,
    )
    blocks = blocks.transpose(0, 2, 4, 1, 3, 5, 6)
    return blocks.reshape(-1, window_size**3, features)


def cells_of(blocks, depth_count, row_count, col_count, window_size):
    features = blocks.shape[-1]
    cells = blocks.reshape(
        depth_count // window_size,
        row_count // window_size,
        col_count // window_size,
        window_size,
        window_size,
        window_size,
        features,
    )
    cells = cells.transpose(0, 3, 1, 4, 2, 5, 6)
    return cells.reshape(depth_count, row_count, col_count, features)


def normalize(cells, gain_row):
    values = cells.astype(jnp.float32)
    center = values - jnp.mean(values, axis=-1, keepdims=True)
    inverse = lax.rsqrt(jnp.mean(center * center, axis=-1, keepdims=True) + EPSILON)
    normed = center * inverse
    return ((normed * gain_row).astype(jnp.bfloat16), normed, inverse)


def norm_back(d_normed, normed, inverse, gain_row):
    scaled = d_normed * gain_row
    mean_first = jnp.mean(scaled, axis=-1, keepdims=True)
    mean_second = jnp.mean(scaled * normed, axis=-1, keepdims=True)
    return inverse * (scaled - mean_first - normed * mean_second)


def region(position, extent, window_size):
    return (position >= extent - window_size).astype(jnp.int32) + (
        position >= extent - window_size // 2
    ).astype(jnp.int32)


def attention_weights(query_rows, key_rows, region_ids, scale):
    scores = (
        jnp.einsum("qhd,khd->hqk", query_rows, key_rows, preferred_element_type=jnp.float32) * scale
    )
    allowed = region_ids[:, None] == region_ids[None, :]
    scores = jnp.where(allowed[None], scores, MASKED)
    row_max = jnp.max(scores, axis=-1, keepdims=True)
    powers = jnp.exp(scores - row_max)
    return powers / jnp.sum(powers, axis=-1, keepdims=True)


def window_forward(packed, region_ids, head_count):
    split = packed.reshape(packed.shape[0], 3, head_count, -1)
    scale = split.shape[-1] ** (-0.5)
    weights = attention_weights(split[:, 0], split[:, 1], region_ids, scale)
    rounded = weights.astype(jnp.bfloat16)
    attended = jnp.einsum("hqk,khd->qhd", rounded, split[:, 2], preferred_element_type=jnp.float32)
    return attended.astype(jnp.bfloat16).reshape(packed.shape[0], -1)


def window_backward(packed, region_ids, d_attended, head_count):
    split = packed.reshape(packed.shape[0], 3, head_count, -1)
    scale = split.shape[-1] ** (-0.5)
    query_rows, key_rows, value_rows = (split[:, 0], split[:, 1], split[:, 2])
    weights = attention_weights(query_rows, key_rows, region_ids, scale)
    rounded = weights.astype(jnp.bfloat16)
    d_output = d_attended.reshape(query_rows.shape)
    d_weights = jnp.einsum("qhd,khd->hqk", d_output, value_rows, preferred_element_type=jnp.float32)
    d_values = jnp.einsum("hqk,qhd->khd", rounded, d_output, preferred_element_type=jnp.float32)
    d_scores = weights * (d_weights - jnp.sum(d_weights * weights, axis=-1, keepdims=True))
    d_scaled = (d_scores * scale).astype(jnp.bfloat16)
    d_query = jnp.einsum("hqk,khd->qhd", d_scaled, key_rows, preferred_element_type=jnp.float32)
    d_keys = jnp.einsum("hqk,qhd->khd", d_scaled, query_rows, preferred_element_type=jnp.float32)
    stacked = jnp.stack([d_query, d_keys, d_values], axis=1)
    return stacked.astype(jnp.bfloat16).reshape(packed.shape[0], -1)


def block_forward(cells, gain_row, qkv_matrix, id_cells, window_size, head_count):
    depth_count, row_count, col_count, features = cells.shape
    normed_b, normed, inverse = normalize(cells, gain_row)
    packed = jnp.dot(
        normed_b.reshape(-1, features), qkv_matrix, preferred_element_type=jnp.float32
    ).astype(jnp.bfloat16)
    packed_win = windows_of(packed.reshape(depth_count, row_count, col_count, -1), window_size)
    ids_win = windows_of(id_cells, window_size)[..., 0]
    attended_win = lax.map(
        lambda window: window_forward(window[0], window[1], head_count), (packed_win, ids_win)
    )
    attended = cells_of(attended_win, depth_count, row_count, col_count, window_size).reshape(
        -1, features
    )
    return (normed_b, normed, inverse, packed_win, ids_win, attended)


def block_backward(state, cot_cells, qkv_matrix, proj_matrix, window_size, head_count):
    normed_b, normed, inverse, packed_win, ids_win, attended = state
    depth_count, row_count, col_count, features = cot_cells.shape
    cot_flat = cot_cells.reshape(-1, features)
    d_attended = jnp.dot(cot_flat, proj_matrix.T, preferred_element_type=jnp.float32).astype(
        jnp.bfloat16
    )
    proj_sum = jnp.dot(attended.T, cot_flat, preferred_element_type=jnp.float32)
    d_att_win = windows_of(
        d_attended.reshape(depth_count, row_count, col_count, features), window_size
    )
    d_packed_win = lax.map(
        lambda window: window_backward(window[0], window[1], window[2], head_count),
        (packed_win, ids_win, d_att_win),
    )
    d_packed = cells_of(d_packed_win, depth_count, row_count, col_count, window_size).reshape(
        -1, 3 * features
    )
    qkv_sum = jnp.dot(
        normed_b.reshape(-1, features).T, d_packed, preferred_element_type=jnp.float32
    )
    d_normed = jnp.dot(d_packed, qkv_matrix.T, preferred_element_type=jnp.float32).reshape(
        depth_count, row_count, col_count, features
    )
    gain_sum = jnp.sum(d_normed * normed, axis=(0, 1, 2))
    return (d_normed, gain_sum, qkv_sum, proj_sum)


def roll_ahead(first_grid, second_grid, half_span):
    first_grid = jnp.roll(first_grid, -half_span, axis=0)
    second_grid = jnp.roll(second_grid, -half_span, axis=0)
    rows_in = passed_along((first_grid[:, :half_span], second_grid[:, :half_span]), "gy", -1)
    first_grid = jnp.concatenate([first_grid[:, half_span:], rows_in[0]], axis=1)
    second_grid = jnp.concatenate([second_grid[:, half_span:], rows_in[1]], axis=1)
    cols_in = passed_along((first_grid[:, :, :half_span], second_grid[:, :, :half_span]), "gx", -1)
    first_grid = jnp.concatenate([first_grid[:, :, half_span:], cols_in[0]], axis=2)
    second_grid = jnp.concatenate([second_grid[:, :, half_span:], cols_in[1]], axis=2)
    return (first_grid, second_grid)


def return_normed(gradient, half_span):
    row_count = gradient.shape[1]
    col_count = gradient.shape[2]
    rows_in = passed_along(
        gradient[:, row_count - half_span :].astype(jnp.bfloat16), "gy", 1
    ).astype(jnp.float32)
    gradient = jnp.concatenate([rows_in, gradient[:, : row_count - half_span]], axis=1)
    cols_in = passed_along(
        gradient[:, :, col_count - half_span :].astype(jnp.bfloat16), "gx", 1
    ).astype(jnp.float32)
    gradient = jnp.concatenate([cols_in, gradient[:, :, : col_count - half_span]], axis=2)
    return jnp.roll(gradient, half_span, axis=0)


def local(tokens, cotangent, gains, qkv_weight, proj_weight):
    depth_count, row_count, col_count, features = tokens.shape
    window_size = WIN
    half_span = window_size // 2
    head_count = HEADS
    total_rows = row_count * lax.axis_size("gy")
    total_cols = col_count * lax.axis_size("gx")
    factor = (depth_count * total_rows * total_cols // 16) ** (-0.5)
    zero_ids = jnp.zeros((depth_count, row_count, col_count, 1), jnp.int32)
    state_zero = block_forward(tokens, gains[0], qkv_weight[0], zero_ids, window_size, head_count)
    branch = jnp.dot(state_zero[5], proj_weight[0], preferred_element_type=jnp.float32).reshape(
        tokens.shape
    )
    middle = (tokens.astype(jnp.float32) + branch).astype(jnp.bfloat16)
    moved, cot_moved = roll_ahead(middle, cotangent, half_span)
    depth_pos = jnp.arange(depth_count, dtype=jnp.int32)
    row_pos = lax.axis_index("gy") * row_count + jnp.arange(row_count, dtype=jnp.int32)
    col_pos = lax.axis_index("gx") * col_count + jnp.arange(col_count, dtype=jnp.int32)
    shifted_ids = (
        9 * region(depth_pos, depth_count, window_size)[:, None, None]
        + 3 * region(row_pos, total_rows, window_size)[None, :, None]
        + region(col_pos, total_cols, window_size)[None, None, :]
    )[..., None]
    state_one = block_forward(moved, gains[1], qkv_weight[1], shifted_ids, window_size, head_count)
    d_normed_one, gain_one, qkv_one, proj_one = block_backward(
        state_one, cot_moved, qkv_weight[1], proj_weight[1], window_size, head_count
    )
    d_returned = return_normed(d_normed_one, half_span)
    plain_norm = normalize(middle, gains[1])
    d_branch_one = norm_back(d_returned, plain_norm[1], plain_norm[2], gains[1])
    grad_mid = (cotangent.astype(jnp.float32) + d_branch_one).astype(jnp.bfloat16)
    d_normed_zero, gain_zero, qkv_zero, proj_zero = block_backward(
        state_zero, grad_mid, qkv_weight[0], proj_weight[0], window_size, head_count
    )
    d_branch_zero = norm_back(d_normed_zero, state_zero[1], state_zero[2], gains[0])
    grad_tokens = grad_mid.astype(jnp.float32) + d_branch_zero
    gain_total, qkv_total, proj_total = lax.psum(
        (
            jnp.stack([gain_zero, gain_one]),
            jnp.stack([qkv_zero, qkv_one]),
            jnp.stack([proj_zero, proj_one]),
        ),
        ("gy", "gx"),
    )
    return (grad_tokens, gain_total * factor, qkv_total * factor, proj_total * factor)


def solution(mesh):
    in_specs = (P(None, "gy", "gx", None), P(None, "gy", "gx", None), P(), P(), P())
    out_specs = (P(None, "gy", "gx", None), P(), P(), P())
    return jax.shard_map(local, mesh=mesh, in_specs=in_specs, out_specs=out_specs, check_vma=False)
```

profile of v0, /device:TPU:1, one launch (start us, length us, event | category | flops | bytes accessed | tf_op | source)
XLA Modules:
  0.0 703.7 jit_solution(1060058887484659785)
XLA Ops:
  25.2 35.8 %while.40 = (s32[]{:T(128)}, bf16[4,512,192]{1,2,0:T(8,128)(2,1)}, bf16[4,512,576]{1,2,0:T(8,128)(2,1)S(1)}, s32[]{:T(128)}) while((s32[]{:T(128)}, bf16[4,512,192]{1,2,0:T(8,128)(2,1)}, bf16[4,512,576]{1,2,0:T(8,128)(2,1)S(1)}, s32[]{:T(128)}) %tuple.94), condition=%wide.region_5.6_spmd, body=%wide.region_2.5_spmd.sunk | while | flops 209289728 | bytes 14970949 | solution.py:116
  25.2 4.8 fusion.225
  30.0 3.4 fusion.226
  34.2 4.8 fusion.225
  43.1 4.8 fusion.225
  52.1 4.8 fusion.225
  75.0 6.2 collective-permute-start.3
  102.7 143.2 %while.41 = (s32[]{:T(128)}, bf16[4,512,576]{1,2,0:T(8,128)(2,1)}, bf16[4,512,576]{1,2,0:T(8,128)(2,1)S(1)}, s32[4,512]{1,0:T(4,128)S(1)}, bf16[4,512,192]{1,2,0:T(8,128)(2,1)}, /*index=5*/s32[]{:T(128)}) while((s32[]{:T(128)}, bf16[4,512,576]{1,2,0:T(8,128)(2,1)}, bf16[4,512,576]{1,2,0:T(8,128)(2,1)S(1)}, s32[4,512]{1,0:T(4,128)S(1)}, ...), condition=%wide.region_14.15_spmd, body=%wide.region_10.14_spmd.sunk | while | flops 535928320 | bytes 75774072 | solution.py:136
  104.0 5.1 fusion.232
  109.1 3.8 fusion.233
  112.9 3.7 fusion.234
  116.6 10.8 %fusion.236 = bf16[512,1,6,32]{0,3,2,1:T(8,128)(2,1)S(1)} fusion(f32[6,512,512]{1,2,0:T(8,128)} %fusion.234, bf16[512,3,6,32]{0,3,2,1:T(8,128)(2,1)S(1)} %bitcast.345, f32[6,512,512]{1,2,0:T(8,128)} %get-tuple-element.296, f32[6,512]{1,0:T(8,128)S(1)} %get-tuple-element.297), kind=kOutput, calls=%fused_computation.37.clone.1 | convolution fusion | flops 111775232 | bytes 25591808 | tf_op jit(solution)/shard_map/while/body/eval_jaxpr/hqk,khd->qhd/dot_general | solution.py:102
  127.4 10.2 %fusion.235 = bf16[512,1,6,32]{0,3,2,1:T(8,128)(2,1)S(1)} fusion(f32[6,512,512]{1,2,0:T(8,128)} %fusion.234, bf16[512,3,6,32]{0,3,2,1:T(8,128)(2,1)S(1)} %bitcast.346, f32[6,512,512]{1,2,0:T(8,128)} %get-tuple-element.296, f32[6,512]{1,0:T(8,128)} %copy-done.42), kind=kOutput, calls=%fused_computation.36.clone.1 | convolution fusion | flops 111775232 | bytes 25591808 | tf_op jit(solution)/shard_map/while/body/eval_jaxpr/hqk,qhd->khd/dot_general | solution.py:103
  139.8 5.1 fusion.232
  144.9 3.8 fusion.233
  148.7 3.7 fusion.234
  152.4 10.8 %fusion.236 = bf16[512,1,6,32]{0,3,2,1:T(8,128)(2,1)S(1)} fusion(f32[6,512,512]{1,2,0:T(8,128)} %fusion.234, bf16[512,3,6,32]{0,3,2,1:T(8,128)(2,1)S(1)} %bitcast.345, f32[6,512,512]{1,2,0:T(8,128)} %get-tuple-element.296, f32[6,512]{1,0:T(8,128)S(1)} %get-tuple-element.297), kind=kOutput, calls=%fused_computation.37.clone.1 | convolution fusion | flops 111775232 | bytes 25591808 | tf_op jit(solution)/shard_map/while/body/eval_jaxpr/hqk,khd->qhd/dot_general | solution.py:102
  163.2 10.2 %fusion.235 = bf16[512,1,6,32]{0,3,2,1:T(8,128)(2,1)S(1)} fusion(f32[6,512,512]{1,2,0:T(8,128)} %fusion.234, bf16[512,3,6,32]{0,3,2,1:T(8,128)(2,1)S(1)} %bitcast.346, f32[6,512,512]{1,2,0:T(8,128)} %get-tuple-element.296, f32[6,512]{1,0:T(8,128)} %copy-done.42), kind=kOutput, calls=%fused_computation.36.clone.1 | convolution fusion | flops 111775232 | bytes 25591808 | tf_op jit(solution)/shard_map/while/body/eval_jaxpr/hqk,qhd->khd/dot_general | solution.py:103
  175.6 5.1 fusion.232
  180.7 3.8 fusion.233
  184.5 3.7 fusion.234
  188.2 10.8 %fusion.236 = bf16[512,1,6,32]{0,3,2,1:T(8,128)(2,1)S(1)} fusion(f32[6,512,512]{1,2,0:T(8,128)} %fusion.234, bf16[512,3,6,32]{0,3,2,1:T(8,128)(2,1)S(1)} %bitcast.345, f32[6,512,512]{1,2,0:T(8,128)} %get-tuple-element.296, f32[6,512]{1,0:T(8,128)S(1)} %get-tuple-element.297), kind=kOutput, calls=%fused_computation.37.clone.1 | convolution fusion | flops 111775232 | bytes 25591808 | tf_op jit(solution)/shard_map/while/body/eval_jaxpr/hqk,khd->qhd/dot_general | solution.py:102
  199.0 10.2 %fusion.235 = bf16[512,1,6,32]{0,3,2,1:T(8,128)(2,1)S(1)} fusion(f32[6,512,512]{1,2,0:T(8,128)} %fusion.234, bf16[512,3,6,32]{0,3,2,1:T(8,128)(2,1)S(1)} %bitcast.346, f32[6,512,512]{1,2,0:T(8,128)} %get-tuple-element.296, f32[6,512]{1,0:T(8,128)} %copy-done.42), kind=kOutput, calls=%fused_computation.36.clone.1 | convolution fusion | flops 111775232 | bytes 25591808 | tf_op jit(solution)/shard_map/while/body/eval_jaxpr/hqk,qhd->khd/dot_general | solution.py:103
  211.4 5.1 fusion.232
  216.5 3.8 fusion.233
  220.3 3.7 fusion.234
  224.0 10.8 %fusion.236 = bf16[512,1,6,32]{0,3,2,1:T(8,128)(2,1)S(1)} fusion(f32[6,512,512]{1,2,0:T(8,128)} %fusion.234, bf16[512,3,6,32]{0,3,2,1:T(8,128)(2,1)S(1)} %bitcast.345, f32[6,512,512]{1,2,0:T(8,128)} %get-tuple-element.296, f32[6,512]{1,0:T(8,128)S(1)} %get-tuple-element.297), kind=kOutput, calls=%fused_computation.37.clone.1 | convolution fusion | flops 111775232 | bytes 25591808 | tf_op jit(solution)/shard_map/while/body/eval_jaxpr/hqk,khd->qhd/dot_general | solution.py:102
  234.8 10.2 %fusion.235 = bf16[512,1,6,32]{0,3,2,1:T(8,128)(2,1)S(1)} fusion(f32[6,512,512]{1,2,0:T(8,128)} %fusion.234, bf16[512,3,6,32]{0,3,2,1:T(8,128)(2,1)S(1)} %bitcast.346, f32[6,512,512]{1,2,0:T(8,128)} %get-tuple-element.296, f32[6,512]{1,0:T(8,128)} %copy-done.42), kind=kOutput, calls=%fused_computation.36.clone.1 | convolution fusion | flops 111775232 | bytes 25591808 | tf_op jit(solution)/shard_map/while/body/eval_jaxpr/hqk,qhd->khd/dot_general | solution.py:103
  245.9 4.5 copy.73
  250.4 3.9 fusion.136
  257.7 38.1 %while.43 = (s32[]{:T(128)}, bf16[4,512,192]{1,2,0:T(8,128)(2,1)}, bf16[4,512,576]{1,2,0:T(8,128)(2,1)S(1)}, s32[4,512]{1,0:T(4,128)S(1)}, s32[]{:T(128)}) while((s32[]{:T(128)}, bf16[4,512,192]{1,2,0:T(8,128)(2,1)}, bf16[4,512,576]{1,2,0:T(8,128)(2,1)S(1)}, s32[4,512]{1,0:T(4,128)S(1)}, s32[]{:T(128)}) %tuple.111), condition=%wide.region_31.32_spmd, body=%wide.region_28.31_spmd.sunk | while | flops 211124736 | bytes 15501393 | solution.py:116
  258.0 5.1 fusion.247
  267.5 5.1 fusion.247
  272.6 3.4 fusion.248
  277.0 5.1 fusion.247
  282.1 3.4 fusion.248
  286.6 5.1 fusion.247
  295.8 3.6 copy.74
  308.2 5.2 collective-permute-done.5
  322.1 141.4 %while.42 = (s32[]{:T(128)}, bf16[4,512,576]{1,2,0:T(8,128)(2,1)}, bf16[4,512,576]{1,2,0:T(8,128)(2,1)}, bf16[4,512,192]{1,2,0:T(8,128)(2,1)}, s32[]{:T(128)}) while((s32[]{:T(128)}, bf16[4,512,576]{1,2,0:T(8,128)(2,1)}, bf16[4,512,576]{1,2,0:T(8,128)(2,1)}, bf16[4,512,192]{1,2,0:T(8,128)(2,1)}, s32[]{:T(128)}) %tuple.109), condition=%wide.region_21.22_spmd, body=%wide.region_17.21_spmd.sunk | while | flops 534093312 | bytes 75194448 | solution.py:136
  324.2 3.7 fusion.244
  327.9 4.8 fusion.242
  332.7 3.8 fusion.243
  336.5 10.8 %fusion.246 = bf16[512,1,6,32]{0,3,2,1:T(8,128)(2,1)S(1)} fusion(f32[6,512,512]{1,2,0:T(8,128)} %fusion.244, bf16[512,3,6,32]{0,3,2,1:T(8,128)(2,1)S(1)} %bitcast.349, f32[6,512,512]{1,2,0:T(8,128)} %get-tuple-element.302, f32[6,512]{1,0:T(8,128)S(1)} %get-tuple-element.303), kind=kOutput, calls=%fused_computation.75.clone.1 | convolution fusion | flops 111775232 | bytes 25591808 | tf_op jit(solution)/shard_map/while/body/eval_jaxpr/hqk,khd->qhd/dot_general | solution.py:102
  347.3 9.3 %fusion.245 = bf16[512,1,6,32]{0,3,2,1:T(8,128)(2,1)S(1)} fusion(f32[6,512,512]{1,2,0:T(8,128)} %fusion.244, bf16[512,3,6,32]{0,3,2,1:T(8,128)(2,1)S(1)} %bitcast.350, f32[6,512,512]{1,2,0:T(8,128)} %get-tuple-element.302, f32[6,512]{1,0:T(8,128)S(1)} %get-tuple-element.303), kind=kOutput, calls=%fused_computation.74.clone.1 | convolution fusion | flops 111775232 | bytes 25591808 | tf_op jit(solution)/shard_map/while/body/eval_jaxpr/hqk,qhd->khd/dot_general | solution.py:103
  359.5 3.7 fusion.244
  363.2 4.8 fusion.242
  368.0 3.8 fusion.243
  371.8 10.8 %fusion.246 = bf16[512,1,6,32]{0,3,2,1:T(8,128)(2,1)S(1)} fusion(f32[6,512,512]{1,2,0:T(8,128)} %fusion.244, bf16[512,3,6,32]{0,3,2,1:T(8,128)(2,1)S(1)} %bitcast.349, f32[6,512,512]{1,2,0:T(8,128)} %get-tuple-element.302, f32[6,512]{1,0:T(8,128)S(1)} %get-tuple-element.303), kind=kOutput, calls=%fused_computation.75.clone.1 | convolution fusion | flops 111775232 | bytes 25591808 | tf_op jit(solution)/shard_map/while/body/eval_jaxpr/hqk,khd->qhd/dot_general | solution.py:102
  382.6 9.3 %fusion.245 = bf16[512,1,6,32]{0,3,2,1:T(8,128)(2,1)S(1)} fusion(f32[6,512,512]{1,2,0:T(8,128)} %fusion.244, bf16[512,3,6,32]{0,3,2,1:T(8,128)(2,1)S(1)} %bitcast.350, f32[6,512,512]{1,2,0:T(8,128)} %get-tuple-element.302, f32[6,512]{1,0:T(8,128)S(1)} %get-tuple-element.303), kind=kOutput, calls=%fused_computation.74.clone.1 | convolution fusion | flops 111775232 | bytes 25591808 | tf_op jit(solution)/shard_map/while/body/eval_jaxpr/hqk,qhd->khd/dot_general | solution.py:103
  394.9 3.7 fusion.244
  398.6 4.8 fusion.242
  403.4 3.8 fusion.243
  407.2 10.8 %fusion.246 = bf16[512,1,6,32]{0,3,2,1:T(8,128)(2,1)S(1)} fusion(f32[6,512,512]{1,2,0:T(8,128)} %fusion.244, bf16[512,3,6,32]{0,3,2,1:T(8,128)(2,1)S(1)} %bitcast.349, f32[6,512,512]{1,2,0:T(8,128)} %get-tuple-element.302, f32[6,512]{1,0:T(8,128)S(1)} %get-tuple-element.303), kind=kOutput, calls=%fused_computation.75.clone.1 | convolution fusion | flops 111775232 | bytes 25591808 | tf_op jit(solution)/shard_map/while/body/eval_jaxpr/hqk,khd->qhd/dot_general | solution.py:102
  418.0 9.3 %fusion.245 = bf16[512,1,6,32]{0,3,2,1:T(8,128)(2,1)S(1)} fusion(f32[6,512,512]{1,2,0:T(8,128)} %fusion.244, bf16[512,3,6,32]{0,3,2,1:T(8,128)(2,1)S(1)} %bitcast.350, f32[6,512,512]{1,2,0:T(8,128)} %get-tuple-element.302, f32[6,512]{1,0:T(8,128)S(1)} %get-tuple-element.303), kind=kOutput, calls=%fused_computation.74.clone.1 | convolution fusion | flops 111775232 | bytes 25591808 | tf_op jit(solution)/shard_map/while/body/eval_jaxpr/hqk,qhd->khd/dot_general | solution.py:103
  430.3 3.7 fusion.244
  433.9 4.8 fusion.242
  438.7 3.8 fusion.243
  442.5 10.8 %fusion.246 = bf16[512,1,6,32]{0,3,2,1:T(8,128)(2,1)S(1)} fusion(f32[6,512,512]{1,2,0:T(8,128)} %fusion.244, bf16[512,3,6,32]{0,3,2,1:T(8,128)(2,1)S(1)} %bitcast.349, f32[6,512,512]{1,2,0:T(8,128)} %get-tuple-element.302, f32[6,512]{1,0:T(8,128)S(1)} %get-tuple-element.303), kind=kOutput, calls=%fused_computation.75.clone.1 | convolution fusion | flops 111775232 | bytes 25591808 | tf_op jit(solution)/shard_map/while/body/eval_jaxpr/hqk,khd->qhd/dot_general | solution.py:102
  453.4 9.3 %fusion.245 = bf16[512,1,6,32]{0,3,2,1:T(8,128)(2,1)S(1)} fusion(f32[6,512,512]{1,2,0:T(8,128)} %fusion.244, bf16[512,3,6,32]{0,3,2,1:T(8,128)(2,1)S(1)} %bitcast.350, f32[6,512,512]{1,2,0:T(8,128)} %get-tuple-element.302, f32[6,512]{1,0:T(8,128)S(1)} %get-tuple-element.303), kind=kOutput, calls=%fused_computation.74.clone.1 | convolution fusion | flops 111775232 | bytes 25591808 | tf_op jit(solution)/shard_map/while/body/eval_jaxpr/hqk,qhd->khd/dot_general | solution.py:103
  463.6 4.7 copy.79
  468.4 4.5 fusion.142
  476.2 68.6 %psum.21 = f32[2,192]{1,0:T(2,128)S(1)} all-reduce(f32[2,192]{1,0:T(2,128)S(1)} %pad_maximum_fusion.11), channel_id=1, replica_groups=mesh['gy'=16,'gx'=8] {'gy','gx'}, use_global_device_ids=true, to_apply=%region_26.27 | all-reduce | flops 384 | bytes 3072 | tf_op jit(solution)/shard_map/psum | solution.py:215
  551.7 140.7 %all-reduce.3.cloned.1.call-done = (f32[2,192,576]{2,1,0:T(8,128)}, f32[2,192,192]{2,1,0:T(8,128)}) async-done(((f32[2,192,576]{2,1,0:T(8,128)}, f32[2,192,192]{2,1,0:T(8,128)}), (f32[2,192,576]{2,1,0:T(8,128)}, f32[2,192,192]{2,1,0:T(8,128)})) %all-reduce.3.cloned.1.call-update) | async-done | bytes 1179664 | tf_op jit(solution)/shard_map/psum | solution.py:215
  (251 shorter events, 132.6 us)
Async XLA Ops:
  7.2 4.0 copy-start.40
  7.2 4.0 copy-start.5
  7.2 685.2 %all-reduce.3.cloned.1.call-start = ((), (), s32[]{:S(2)}) async-start(), calls=%async_computation | async-start | bytes 2752512 | tf_op jit(solution)/shard_map/psum | solution.py:215
  9.8 4.3 copy-start.25
  9.8 64.3 %collective-permute-start.2 = (bf16[8,4,32,192]{3,2,1,0:T(8,128)(2,1)}, bf16[8,4,32,192]{3,2,1,0:T(8,128)(2,1)}, u32[]{:S(2)}, u32[]{:S(2)}) collective-permute-start(bf16[8,4,32,192]{3,2,1,0:T(8,128)(2,1)} %get-tuple-element.178), channel_id=1, source_target_pairs={{0,120},{8,0},{16,8},{24,16},{32,24},{40,32},{48,40},{56,48},{64,5... | collective-permute-start | bytes 1179656 | tf_op jit(solution)/shard_map/ppermute | solution.py:17
  11.2 1.8 copy-start.38
  11.2 78.0 %copy-start.36 = (f32[1,192]{1,0:T(1,128)}, f32[1,192]{1,0:T(1,128)S(1)}, u32[]{:S(2)}) copy-start(f32[1,192]{1,0:T(1,128)S(1)} %get-tuple-element.185) | copy-start | bytes 2308
  11.6 1.4 copy-start.21
  12.3 0.8 copy-start.29
  13.1 1.0 copy-start.13
  61.0 4.8 copy-start
  65.8 5.2 copy-start.3
  65.9 8.2 %copy-start.10 = (bf16[8,4,32,192]{3,2,1,0:T(8,128)(2,1)S(1)}, bf16[8,4,32,192]{3,2,1,0:T(8,128)(2,1)}, u32[]{:S(2)}) copy-start(bf16[8,4,32,192]{3,2,1,0:T(8,128)(2,1)} %get-tuple-element.177) | copy-start | bytes 1179652
  66.9 14.3 %collective-permute-start = (bf16[8,4,32,192]{3,2,1,0:T(8,128)(2,1)}, bf16[8,4,32,192]{3,2,1,0:T(8,128)(2,1)S(1)}, u32[]{:S(2)}, u32[]{:S(2)}) collective-permute-start(bf16[8,4,32,192]{3,2,1,0:T(8,128)(2,1)} %get-tuple-element.182), channel_id=1, source_target_pairs={{0,120},{8,0},{16,8},{24,16},{32,24},{40,32},{48,40},{56,48},{64,5... | collective-permute-start | bytes 1179656 | tf_op jit(solution)/shard_map/ppermute | solution.py:17
  70.2 11.1 %copy-start.23 = (f32[8,8,32]{2,1,0:T(8,128)}, f32[8,8,32]{2,1,0:T(8,128)S(1)}, u32[]{:S(2)}) copy-start(f32[8,8,32]{2,1,0:T(8,128)S(1)} %broadcast_multiply_fusion.7) | copy-start | bytes 24580
  75.0 9.0 %collective-permute-start.3 = (bf16[8,8,4,192]{3,2,1,0:T(4,128)(2,1)S(1)}, bf16[8,8,4,192]{3,2,1,0:T(4,128)(2,1)S(1)}, u32[]{:S(2)}, u32[]{:S(2)}) collective-permute-start(bf16[8,8,4,192]{3,2,1,0:T(4,128)(2,1)S(1)} %pad_maximum_fusion.9), channel_id=1, source_target_pairs={{0,7},{1,0},{2,1},{3,2},{4,3},{5,4},{6,5},{7,6},{8,15},{9,8},{10,9... | collective-permute-start | bytes 294920 | tf_op jit(solution)/shard_map/ppermute | solution.py:17
  81.3 6.7 collective-permute-start.1
  83.6 1.7 copy-start.33
  84.0 5.2 copy-start.1
  84.4 1.0 copy-start.8
  87.9 3.0 copy-start.26
  87.9 5.3 copy-start.17
  88.3 1.6 copy-start.32
  89.2 0.8 copy-start.35
  89.9 1.0 copy-start.11
  109.1 7.5 %copy-start.42 = (f32[6,512]{1,0:T(8,128)}, f32[6,512]{1,0:T(8,128)S(1)}, u32[]{:S(2)}) copy-start(f32[6,512]{1,0:T(8,128)S(1)} %get-tuple-element.297) | copy-start | bytes 36868 | tf_op jit(solution)/shard_map/while
  144.9 7.5 %copy-start.42 = (f32[6,512]{1,0:T(8,128)}, f32[6,512]{1,0:T(8,128)S(1)}, u32[]{:S(2)}) copy-start(f32[6,512]{1,0:T(8,128)S(1)} %get-tuple-element.297) | copy-start | bytes 36868 | tf_op jit(solution)/shard_map/while
  180.7 7.5 %copy-start.42 = (f32[6,512]{1,0:T(8,128)}, f32[6,512]{1,0:T(8,128)S(1)}, u32[]{:S(2)}) copy-start(f32[6,512]{1,0:T(8,128)S(1)} %get-tuple-element.297) | copy-start | bytes 36868 | tf_op jit(solution)/shard_map/while
  216.5 7.5 %copy-start.42 = (f32[6,512]{1,0:T(8,128)}, f32[6,512]{1,0:T(8,128)S(1)}, u32[]{:S(2)}) copy-start(f32[6,512]{1,0:T(8,128)S(1)} %get-tuple-element.297) | copy-start | bytes 36868 | tf_op jit(solution)/shard_map/while
  245.9 4.5 copy-start.2
  245.9 4.5 copy-start.18
  254.3 1.3 copy-start.19
  256.5 48.0 %collective-permute-start.4 = (bf16[8,4,32,192]{3,2,1,0:T(8,128)(2,1)}, bf16[8,4,32,192]{3,2,1,0:T(8,128)(2,1)}, u32[]{:S(2)}, u32[]{:S(2)}) collective-permute-start(bf16[8,4,32,192]{3,2,1,0:T(8,128)(2,1)} %slice.284), channel_id=1, source_target_pairs={{0,8},{8,16},{16,24},{24,32},{32,40},{40,48},{48,56},{56,64},{64,7... | collective-permute-start | bytes 1179656 | tf_op jit(solution)/shard_map/ppermute | solution.py:17
  295.8 3.7 copy-start.20
  299.4 1.7 copy-start.12
  304.5 3.2 copy-start.9
  305.9 7.5 %collective-permute-start.5 = (bf16[8,8,4,192]{3,2,1,0:T(4,128)(2,1)S(1)}, bf16[8,8,4,192]{3,2,1,0:T(4,128)(2,1)S(1)}, u32[]{:S(2)}, u32[]{:S(2)}) collective-permute-start(bf16[8,8,4,192]{3,2,1,0:T(4,128)(2,1)S(1)} %fusion.153), channel_id=1, source_target_pairs={{0,1},{1,2},{2,3},{3,4},{4,5},{5,6},{6,7},{7,0},{8,9},{9,10},{10,1... | collective-permute-start | bytes 294920 | tf_op jit(solution)/shard_map/ppermute | solution.py:17
  313.8 1.2 copy-start.4
  313.8 1.2 copy-start.24
  313.8 1.2 copy-start.31
  313.8 1.2 copy-start.37
  314.1 2.6 copy-start.16
  316.7 1.5 copy-start.34
  463.6 4.7 copy-start.6
  463.6 4.8 copy-start.22
  463.6 4.8 copy-start.27
  463.6 4.8 copy-start.30
  463.6 4.8 copy-start.39
  468.4 4.5 copy-start.7
  472.9 1.2 copy-start.15
  472.9 1.7 copy-start.14
  474.6 1.6 copy-start.41
  474.6 71.1 %copy-start.28 = (f32[1,192,576]{2,1,0:T(8,128)S(1)}, f32[1,192,576]{2,1,0:T(8,128)}, u32[]{:S(2)}) copy-start(f32[1,192,576]{2,1,0:T(8,128)} %convolution_bitcast_fusion) | copy-start | bytes 1327108
Sparse Core Ops, SparseCore 0:
  547.8 144.5 all-reduce.2
where the time goes:
time: 713 us; the launch traced here: 704 us
  matrix products  353 us (50%)
  waiting for transfers between devices  146 us (20%)
  local copies, waits for them, and re-layouts  78.7 us (11%)
  blocking collectives  68.6 us (10%)
  other arithmetic  28.2 us (4%)
  between operations  15.3 us (2%)
  starting transfers between devices  14 us (2%)
    psum x1, waiting for transfers between devices, local(): lax.psum((jnp.stack([gain_zero, gain_one]), jnp.stack([qkv_zero, qkv_one]...  141 us
    dot_general x8, matrix products, window_backward(): jnp.einsum('hqk,khd->qhd', d_scaled, key_rows, preferred_element_type=jnp...  86.4 us
    sub x16, matrix products, attention_weights(): powers = jnp.exp(scores - row_max)  79 us
    dot_general x8, matrix products, window_backward(): jnp.einsum('hqk,qhd->khd', d_scaled, query_rows, preferred_element_type=j...  77.8 us
    psum x1, blocking collectives, local(): lax.psum((jnp.stack([gain_zero, gain_one]), jnp.stack([qkv_zero, qkv_one]...  68.6 us
    dot_general x8, matrix products, window_backward(): jnp.einsum('hqk,qhd->khd', rounded, d_output, preferred_element_type=jnp....  30.6 us
    dot_general x8, matrix products, window_backward(): jnp.einsum('qhd,khd->hqk', d_output, value_rows, preferred_element_type=j...  29.5 us
    dot_general x8, matrix products, window_forward(): jnp.einsum('hqk,khd->qhd', rounded, split[:, 2], preferred_element_type=j...  27.4 us
  transfers between devices with their start and end apart: 7, of which 2 were waited for; matrix products, arithmetic and copies ran while one was open for 17% of the time, Pallas kernels for 0%

commit v1 on v0

v1 whole, which is shorter than its diff:
```python
import functools
import math

import jax
import jax.numpy as jnp
from jax import lax
from jax.experimental import pallas as pl
from jax.experimental.pallas import tpu as pltpu
from jax.sharding import PartitionSpec as P

HEADS = 6
WIN = 8
C = 192
HD = 32
TOK = WIN**3
HALF = TOK // 2
EPSILON = 1e-05
MASKED = -1e30
SCALE = HD**-0.5
LOG2E = 1.0 / math.log(2.0)
LN2 = math.log(2.0)
F32 = jnp.float32
BF16 = jnp.bfloat16
GROUPS = ((0, 1, 2), (3, 4, 5))


def dot(left, right):
    return jnp.dot(left, right, preferred_element_type=F32)


def dot_t(left, right):
    return lax.dot_general(left, right, (((1,), (1,)), ((), ())), preferred_element_type=F32)


def rows(head, part=0):
    start = part * C + head * HD
    return slice(start, start + HD)


def layer_norm(x, gain_row):
    center = x - jnp.sum(x, axis=-1, keepdims=True) * (1.0 / C)
    inverse = lax.rsqrt(jnp.sum(center * center, axis=-1, keepdims=True) * (1.0 / C) + EPSILON)
    normed = center * inverse
    return (normed * gain_row).astype(BF16), normed, inverse


def norm_back(d_normed, normed, inverse, gain_row):
    scaled = d_normed * gain_row
    first = jnp.sum(scaled, axis=-1, keepdims=True) * (1.0 / C)
    second = jnp.sum(scaled * normed, axis=-1, keepdims=True) * (1.0 / C)
    return inverse * (scaled - first - normed * second)


def fold_tokens(x):
    return jnp.sum(x.reshape(TOK // 8, 8, C), axis=0)


def halves(first, second):
    a = first.astype(F32).reshape(TOK // 8, 8, C)
    b = second.astype(F32).reshape(TOK // 8, 8, C)
    place = lax.broadcasted_iota(jnp.int32, (TOK // 8, 8, C), 1)
    return jnp.where(place < 4, a, b).reshape(TOK, C)


def prepare_weights(block, w_ref, p_ref, wt_ref, wkv_ref, pt_ref):
    weight = w_ref[block].astype(F32)
    wt_ref[...] = weight.T.astype(BF16)
    wkv_ref[...] = weight[:, C:].astype(BF16)
    if pt_ref is not None:
        pt_ref[...] = p_ref[block].astype(F32).T.astype(BF16)


def project(normed_b, wt_ref, wkv_ref, qkvt_ref, kv_ref):
    qkvt_ref[:C] = (dot_t(wt_ref[:C], normed_b) * (SCALE * LOG2E)).astype(BF16)
    qkvt_ref[C:] = dot_t(wt_ref[C:], normed_b).astype(BF16)
    kv_ref[...] = dot(normed_b, wkv_ref[...]).astype(BF16)


def regular_forward(group, qkvt_ref, kv_ref, e_ref, r_ref, o_ref):
    s = [dot(kv_ref[:, rows(h)], qkvt_ref[rows(h)]) for h in group]
    m = [jnp.max(x, axis=0, keepdims=True) for x in s]
    ef = [jnp.exp2(x - y) for x, y in zip(s, m)]
    e = [x.astype(BF16) for x in ef]
    for h, x in zip(group, e):
        e_ref[h] = x
    r = [1.0 / jnp.sum(x, axis=0, keepdims=True) for x in ef]
    o = [dot(qkvt_ref[rows(h, 2)], x) for h, x in zip(group, e)]
    for h, x, y in zip(group, o, r):
        o_ref[rows(h)] = x * y
        r_ref[h : h + 1] = y


def regular_backward(group, qkvt_ref, kv_ref, e_ref, r_ref, o_ref, da_ref, dqkvt_ref):
    da = [(da_ref[rows(h)] * r_ref[h : h + 1]).astype(BF16) for h in group]
    d = [
        jnp.sum(x.astype(F32) * o_ref[rows(h)], axis=0, keepdims=True) for h, x in zip(group, da)
    ]
    dp = [dot(kv_ref[:, rows(h, 1)], x) for h, x in zip(group, da)]
    for h, x in zip(group, da):
        dqkvt_ref[rows(h, 2)] = dot_t(x, e_ref[h]).astype(BF16)
    ds = [
        (e_ref[h].astype(F32) * (x - y)).astype(BF16) for h, x, y in zip(group, dp, d)
    ]
    for h, x in zip(group, ds):
        dqkvt_ref[rows(h)] = (dot(qkvt_ref[rows(h, 1)], x) * SCALE).astype(BF16)
        dqkvt_ref[rows(h, 1)] = (dot_t(qkvt_ref[rows(h)], x) * LN2).astype(BF16)


def shifted_both(group, qkvt_ref, kv_ref, bias, o_ref, da_ref, dqkvt_ref):
    parts = [(h, slice(k * HALF, (k + 1) * HALF)) for h in group for k in range(2)]
    s = [dot(kv_ref[t, rows(h)], qkvt_ref[rows(h), t]) + bias for h, t in parts]
    m = [jnp.max(x, axis=0, keepdims=True) for x in s]
    ef = [jnp.exp2(x - y) for x, y in zip(s, m)]
    e = [x.astype(BF16) for x in ef]
    r = [1.0 / jnp.sum(x, axis=0, keepdims=True) for x in ef]
    o = [dot(qkvt_ref[rows(h, 2), t], x) * y for (h, t), x, y in zip(parts, e, r)]
    da = [(da_ref[rows(h), t] * y).astype(BF16) for (h, t), y in zip(parts, r)]
    d = [jnp.sum(x.astype(F32) * y, axis=0, keepdims=True) for x, y in zip(da, o)]
    dp = [dot(kv_ref[t, rows(h, 1)], x) for (h, t), x in zip(parts, da)]
    for (h, t), x, y, z in zip(parts, o, da, e):
        o_ref[rows(h), t] = x.astype(BF16)
        dqkvt_ref[rows(h, 2), t] = dot_t(y, z).astype(BF16)
    ds = [(x.astype(F32) * (y - z)).astype(BF16) for x, y, z in zip(e, dp, d)]
    for (h, t), x in zip(parts, ds):
        dqkvt_ref[rows(h), t] = (dot(qkvt_ref[rows(h, 1), t], x) * SCALE).astype(BF16)
        dqkvt_ref[rows(h, 1), t] = (dot_t(qkvt_ref[rows(h), t], x) * LN2).astype(BF16)


def write_bias(bias_ref):
    last_row = lax.axis_index("gy") == lax.axis_size("gy") - 1
    last_col = lax.axis_index("gx") == lax.axis_size("gx") - 1
    key = lax.broadcasted_iota(jnp.int32, (HALF, HALF), 0)
    query = lax.broadcasted_iota(jnp.int32, (HALF, HALF), 1)
    row_bias = jnp.where((key // 32) % 2 != (query // 32) % 2, MASKED, 0.0).astype(F32)
    col_bias = jnp.where((key // 4) % 2 != (query // 4) % 2, MASKED, 0.0).astype(F32)
    row_bias = row_bias * jnp.where(last_row, 1.0, 0.0).astype(F32)
    col_bias = col_bias * jnp.where(last_col, 1.0, 0.0).astype(F32)
    bias_ref[0] = row_bias
    bias_ref[1] = jnp.minimum(row_bias, col_bias)


def kernel_forward(
    tok_ref, gain_ref, w_ref, p_ref,
    mid_ref, e_ref, r_ref, o_ref, qkvt_ref, kv_ref, nb_ref, normed_ref, inv_ref,
    x32_ref, wt_ref, wkv_ref, pt_ref,
):
    prepare_weights(0, w_ref, p_ref, wt_ref, wkv_ref, pt_ref)
    x32_ref[...] = tok_ref[...].astype(F32)

    def window(w, carry):
        x = x32_ref[:, :, pl.ds(pl.multiple_of(w * WIN, WIN), WIN), :].reshape(TOK, C)
        normed_b, normed, inverse = layer_norm(x, gain_ref[0:1])
        nb_ref[w] = normed_b
        normed_ref[w] = normed
        inv_ref[w] = inverse
        project(normed_b, wt_ref, wkv_ref, qkvt_ref.at[w], kv_ref.at[w])
        for group in GROUPS:
            regular_forward(
                group, qkvt_ref.at[w], kv_ref.at[w], e_ref.at[w], r_ref.at[w], o_ref.at[w]
            )
        branch = dot(pt_ref[...], o_ref[w].astype(BF16)).T
        mid_ref[w] = (x + branch).astype(BF16).reshape(WIN, 64, C)
        return carry

    lax.fori_loop(0, 4, window, 0)


def kernel_shifted(
    mid_ref, cot_ref, gain_ref, w_ref, p_ref,
    grad_ref, wsum_ref, gsum_ref,
    qkvt_ref, kv_ref, o_ref, da_ref, dqkvt_ref, bias_ref, wt_ref, wkv_ref,
):
    prepare_weights(1, w_ref, p_ref, wt_ref, wkv_ref, None)
    write_bias(bias_ref)
    wsum_ref[...] = jnp.zeros_like(wsum_ref)
    gsum_ref[...] = jnp.zeros_like(gsum_ref)

    def window(w, carry):
        x = halves(mid_ref[w + 1], mid_ref[w])
        normed_b, normed, inverse = layer_norm(x, gain_ref[1:2])
        project(normed_b, wt_ref, wkv_ref, qkvt_ref, kv_ref)
        cot = halves(cot_ref[w + 1], cot_ref[w])
        cot_b = cot.astype(BF16)
        da_ref[...] = dot_t(p_ref[1], cot_b)
        bias = bias_ref[w // 3]
        for group in GROUPS:
            shifted_both(group, qkvt_ref, kv_ref, bias, o_ref, da_ref, dqkvt_ref)
        wsum_ref[3 * C :] += dot(o_ref[...], cot_b)
        wsum_ref[: 3 * C] += dot(dqkvt_ref[...], normed_b)
        d_normed = dot(w_ref[1], dqkvt_ref[...]).T
        gsum_ref[...] += fold_tokens(d_normed * normed)
        grad = cot + norm_back(d_normed, normed, inverse, gain_ref[1:2])
        grad_ref[w] = grad.astype(BF16).reshape(WIN, 64, C)
        return carry

    lax.fori_loop(0, 4, window, 0)


def kernel_backward(
    grad_ref, gain_ref, w_ref, p_ref, e_ref, r_ref, o_ref, qkvt_ref, kv_ref, nb_ref, normed_ref, inv_ref,
    out_ref, wsum_ref, gsum_ref,
    da_ref, dqkvt_ref,
):
    wsum_ref[...] = jnp.zeros_like(wsum_ref)
    gsum_ref[...] = jnp.zeros_like(gsum_ref)

    def window(w, carry):
        grad = halves(grad_ref[w], grad_ref[w + 1])
        grad_b = grad.astype(BF16)
        da_ref[...] = dot_t(p_ref[0], grad_b)
        for group in GROUPS:
            regular_backward(
                group, qkvt_ref.at[w], kv_ref.at[w], e_ref.at[w], r_ref.at[w], o_ref.at[w],
                da_ref, dqkvt_ref,
            )
        wsum_ref[3 * C :] += dot(o_ref[w].astype(BF16), grad_b)
        wsum_ref[: 3 * C] += dot(dqkvt_ref[...], nb_ref[w])
        d_normed = dot(w_ref[0], dqkvt_ref[...]).T
        normed = normed_ref[w]
        gsum_ref[...] += fold_tokens(d_normed * normed)
        out = grad + norm_back(d_normed, normed, inv_ref[w], gain_ref[0:1])
        out_ref[:, :, pl.ds(pl.multiple_of(w * WIN, WIN), WIN), :] = out.reshape(WIN, WIN, WIN, C)
        return carry

    lax.fori_loop(0, 4, window, 0)


def call(kernel, outs, scratch, *args, **params):
    whole = pl.BlockSpec(memory_space=pltpu.VMEM)
    return pl.pallas_call(
        kernel,
        out_shape=[jax.ShapeDtypeStruct(*o) for o in outs],
        in_specs=[whole] * len(args),
        out_specs=[whole] * len(outs),
        scratch_shapes=[pltpu.VMEM(*s) for s in scratch],
        compiler_params=pltpu.CompilerParams(vmem_limit_bytes=58 * 2**20, **params),
    )(*args)


def pass_along(value, axis, steps):
    count = lax.axis_size(axis)
    return lax.ppermute(value, axis, [(i, (i + steps) % count) for i in range(count)])


def pull_ahead(grid):
    ahead = jnp.concatenate([pass_along(grid[:, :, :32], "gy", -1), grid[:, :, 32:]], axis=2)
    return jnp.concatenate([ahead, pass_along(ahead[:1], "gx", -1)], axis=0)


def push_back(grid):
    back = jnp.concatenate([pass_along(grid[:, :, :32], "gy", 1), grid[:, :, 32:]], axis=2)
    return jnp.concatenate([pass_along(back[3:], "gx", 1), back], axis=0)


def local(tokens, cotangent, gains, qkv_weight, proj_weight):
    depth_count, row_count, col_count, features = tokens.shape
    total = depth_count * row_count * col_count * lax.axis_size("gy") * lax.axis_size("gx")
    factor = (total // 16) ** (-0.5)
    windows = col_count // WIN
    cot_win = (
        cotangent.reshape(WIN, WIN, windows, WIN, C).transpose(2, 0, 1, 3, 4).reshape(4, WIN, 64, C)
    )
    cot_ahead = pull_ahead(cot_win)
    weights = [((3 * C, C), BF16), ((C, 2 * C), BF16)]
    mid, e, r, o, qkvt, kv, nb, normed, inverse = call(
        kernel_forward,
        [
            ((4, WIN, 64, C), BF16),
            ((4, HEADS, TOK, TOK), BF16),
            ((4, 8, TOK), F32),
            ((4, C, TOK), F32),
            ((4, 3 * C, TOK), BF16),
            ((4, TOK, 2 * C), BF16),
            ((4, TOK, C), BF16),
            ((4, TOK, C), F32),
            ((4, TOK, 1), F32),
        ],
        [((WIN, WIN, 32, C), F32)] + weights + [((C, C), BF16)],
        tokens, gains, qkv_weight, proj_weight,
    )
    mid_ahead = pull_ahead(mid).reshape(5, TOK, C)
    grad, wsum_one, gsum_one = call(
        kernel_shifted,
        [((4, WIN, 64, C), BF16), ((4 * C, C), F32), ((8, C), F32)],
        [
            ((3 * C, TOK), BF16),
            ((TOK, 2 * C), BF16),
            ((C, TOK), BF16),
            ((C, TOK), F32),
            ((3 * C, TOK), BF16),
            ((2, HALF, HALF), F32),
        ]
        + weights,
        mid_ahead, cot_ahead.reshape(5, TOK, C), gains, qkv_weight, proj_weight,
    )
    grad_back = push_back(grad).reshape(5, TOK, C)
    out, wsum_zero, gsum_zero = call(
        kernel_backward,
        [((WIN, WIN, 32, C), F32), ((4 * C, C), F32), ((8, C), F32)],
        [((C, TOK), F32), ((3 * C, TOK), BF16)],
        grad_back, gains, qkv_weight, proj_weight, e, r, o, qkvt, kv, nb, normed, inverse,
    )
    wsum, gsum = lax.psum(
        (jnp.stack([wsum_zero, wsum_one]), jnp.stack([gsum_zero, gsum_one]).sum(1)), ("gy", "gx")
    )
    return (
        out,
        gsum * factor,
        wsum[:, : 3 * C].transpose(0, 2, 1) * factor,
        wsum[:, 3 * C :] * factor,
    )


def solution(mesh):
    in_specs = (P(None, "gy", "gx", None), P(None, "gy", "gx", None), P(), P(), P())
    out_specs = (P(None, "gy", "gx", None), P(), P(), P())
    return jax.shard_map(local, mesh=mesh, in_specs=in_specs, out_specs=out_specs, check_vma=False)
```

time: 713 us -> 285 us (0.40); the launches traced: 704 us -> 284 us
  matrix products: 353 us -> 0 us
  local copies, waits for them, and re-layouts: 78.7 us -> 5.98 us
  Pallas kernels: 0 us -> 65 us
  waiting for transfers between devices: 146 us -> 103 us
  other arithmetic: 28.2 us -> 10.3 us
    dot_general x51 -> x0, matrix products: 274 us -> none  [the longest x8 86.4 us: window_backward(): jnp.einsum('hqk,khd->qhd', d_scaled, key_rows, preferred_element_type=jnp...]
    sub x16 -> x0, matrix products: 79 us -> none  [attention_weights(): powers = jnp.exp(scores - row_max)]
    pallas_call x0 -> x3, Pallas kernels: none -> 65 us  [call(): pl.pallas_call(kernel, out_shape=[jax.ShapeDtypeStruct(*o) for o in outs]...]
    psum x1, waiting for transfers between devices: 141 us -> 82.6 us  [local(): lax.psum((jnp.stack([wsum_zero, wsum_one]), jnp.stack([gsum_zero, gsum_on...]
    while x16 -> x0, local copies, waits for them, and re-layouts: 21.7 us -> none  [the longest x5 14.6 us: block_backward(): lax.map(lambda window: window_backward(window[0], window[1], window[2], h...]
    ppermute x6, waiting for transfers between devices: 5.19 us -> 20.4 us  [pass_along(): lax.ppermute(value, axis, [(i, (i + steps) % count) for i in range(count)])]
    dynamic_update_slice x16 -> x0, local copies, waits for them, and re-layouts: 12.5 us -> none  [the longest x8 6.94 us: block_backward(): lax.map(lambda window: window_backward(window[0], window[1], window[2], h...]
    dynamic_slice x32 -> x0, local copies, waits for them, and re-layouts: 12.5 us -> none  [the longest x8 7.52 us: block_backward(): lax.map(lambda window: window_backward(window[0], window[1], window[2], h...]
  transfers between devices with their start and end apart: 7 -> 7, of which waited for: 2 -> 4; matrix products, arithmetic and copies ran while one was open for 17% -> 1% of each run, Pallas kernels for 0% -> 7%
where the time goes in v1:
time: 285 us; the launch traced here: 284 us
  waiting for transfers between devices  103 us (36%)
  blocking collectives  66 us (23%)
  Pallas kernels  65 us (23%)
  starting transfers between devices  20 us (7%)
  between operations  14.1 us (5%)
  other arithmetic  10.3 us (4%)
  local copies, waits for them, and re-layouts  5.98 us (2%)
    psum x1, waiting for transfers between devices, local(): lax.psum((jnp.stack([wsum_zero, wsum_one]), jnp.stack([gsum_zero, gsum_on...  82.6 us
    psum x1, blocking collectives, local(): lax.psum((jnp.stack([wsum_zero, wsum_one]), jnp.stack([gsum_zero, gsum_on...  66 us
    pallas_call x3, Pallas kernels, call(): pl.pallas_call(kernel, out_shape=[jax.ShapeDtypeStruct(*o) for o in outs]...  65 us
    ppermute x6, waiting for transfers between devices, pass_along(): lax.ppermute(value, axis, [(i, (i + steps) % count) for i in range(count)])  20.4 us
    ppermute x6, starting transfers between devices, pass_along(): lax.ppermute(value, axis, [(i, (i + steps) % count) for i in range(count)])  19.9 us
  transfers between devices with their start and end apart: 7, of which 4 were waited for; matrix products, arithmetic and copies ran while one was open for 1% of the time, Pallas kernels for 7%

profile of v1, /device:TPU:1, one launch (start us, length us, event | category | flops | bytes accessed | tf_op | source)
XLA Modules:
  0.0 284.3 jit_solution(5394710456129220650)
XLA Ops:
  7.2 0.0 copy-start
  7.2 0.0 all-reduce.2.cloned.1.call-start
  7.2 1.2 copy-done
  8.4 0.1 copy_bitcast_fusion
  8.5 0.1 fusion.2
  8.6 1.5 collective-permute-start.2
  10.1 21.1 %shard_map.84 = (bf16[4,8,64,192]{3,2,1,0:T(8,128)(2,1)}, bf16[4,6,512,512]{3,2,1,0:T(8,128)(2,1)}, f32[4,8,512]{2,1,0:T(8,128)}, f32[4,192,512]{2,1,0:T(8,128)}...) custom-call(bf16[8,8,32,192]{3,2,1,0:T(8,128)(2,1)} %tok_ref.1, ...), custom_call_target="tpu_custom_call" | custom-call | tf_op jit(solution)/shard_map/pallas_call | solution.py:230
  31.2 1.3 fusion.3
  32.5 3.4 %collective-permute-start = (bf16[4,8,32,192]{3,2,1,0:T(8,128)(2,1)S(1)}, bf16[4,8,32,192]{3,2,1,0:T(8,128)(2,1)S(1)}, u32[]{:S(2)}, u32[]{:S(2)}) collective-permute-start(bf16[4,8,32,192]{3,2,1,0:T(8,128)(2,1)S(1)} %get-tuple-element.42), channel_id=1, source_target_pairs={{0,120},{8,0},{16,8},{24,16},{32,24},{40,32},{48,40},{56,48},{64,5... | collective-permute-start | bytes 1179656 | tf_op jit(solution)/shard_map/ppermute | solution.py:242
  35.9 0.0 collective-permute-done.2
  35.9 6.2 %collective-permute-start.3 = (bf16[1,8,64,192]{3,2,1,0:T(8,128)(2,1)S(1)}, bf16[1,8,64,192]{3,2,1,0:T(8,128)(2,1)S(1)}, u32[]{:S(2)}, u32[]{:S(2)}) collective-permute-start(bf16[1,8,64,192]{3,2,1,0:T(8,128)(2,1)S(1)} %pad_maximum_fusion.4), channel_id=1, source_target_pairs={{0,7},{1,0},{2,1},{3,2},{4,3},{5,4},{6,5},{7,6},{8,15},{9,8},{10,9... | collective-permute-start | bytes 589832 | tf_op jit(solution)/shard_map/ppermute | solution.py:242
  42.1 0.0 collective-permute-done
  42.1 5.6 %collective-permute-start.1 = (bf16[1,8,64,192]{3,2,1,0:T(8,128)(2,1)S(1)}, bf16[1,8,64,192]{3,2,1,0:T(8,128)(2,1)S(1)}, u32[]{:S(2)}, u32[]{:S(2)}) collective-permute-start(bf16[1,8,64,192]{3,2,1,0:T(8,128)(2,1)S(1)} %pad_maximum_fusion.5), channel_id=1, source_target_pairs={{0,7},{1,0},{2,1},{3,2},{4,3},{5,4},{6,5},{7,6},{8,15},{9,8},{10,9... | collective-permute-start | bytes 589832 | tf_op jit(solution)/shard_map/ppermute | solution.py:242
  47.8 0.0 collective-permute-done.3
  47.8 1.4 pad_maximum_fusion.2
  49.1 2.5 collective-permute-done.1
  51.6 1.4 pad_maximum_fusion.1
  53.0 19.0 %shard_map.85 = (bf16[4,8,64,192]{3,2,1,0:T(8,128)(2,1)}, f32[768,192]{1,0:T(8,128)}, f32[8,192]{1,0:T(8,128)}) custom-call(bf16[5,512,192]{2,1,0:T(8,128)(2,1)} %bitcast.18, bf16[5,512,192]{2,1,0:T(8,128)(2,1)} %bitcast.17, f32[2,192]{1,0:T(2,128)} %gain_ref.5, bf16[2,192,576]{2,1,0:T(8,128)(2,1)} %w_ref.5, bf16[2,192,192]{2,1,0:T(8,128)(2,1)} %p_ref.5), custom_call_target="tpu_custom_call" | custom-call | tf_op jit(solution)/shard_map/pallas_call | solution.py:230
  72.0 1.3 fusion.1
  73.2 1.9 collective-permute-start.4
  75.2 6.1 %collective-permute-done.4 = bf16[4,8,32,192]{3,2,1,0:T(8,128)(2,1)S(1)} collective-permute-done((bf16[4,8,32,192]{3,2,1,0:T(8,128)(2,1)S(1)}, bf16[4,8,32,192]{3,2,1,0:T(8,128)(2,1)S(1)}, u32[]{:S(2)}, u32[]{:S(2)}) %collective-permute-start.4) | collective-permute-done | bytes 393248 | tf_op jit(solution)/shard_map/ppermute | solution.py:242
  81.3 1.4 collective-permute-start.5
  82.7 11.8 %collective-permute-done.5 = bf16[1,8,64,192]{3,2,1,0:T(8,128)(2,1)S(1)} collective-permute-done((bf16[1,8,64,192]{3,2,1,0:T(8,128)(2,1)S(1)}, bf16[1,8,64,192]{3,2,1,0:T(8,128)(2,1)S(1)}, u32[]{:S(2)}, u32[]{:S(2)}) %collective-permute-start.5) | collective-permute-done | bytes 196640 | tf_op jit(solution)/shard_map/ppermute | solution.py:242
  94.5 1.4 maximum_maximum_fusion
  95.9 0.0 copy-start.1
  95.9 24.9 %shard_map.86 = (f32[8,8,32,192]{3,2,1,0:T(8,128)}, f32[768,192]{1,0:T(8,128)}, f32[8,192]{1,0:T(8,128)}) custom-call(bf16[5,512,192]{2,1,0:T(8,128)(2,1)} %bitcast.16, f32[2,192]{1,0:T(2,128)} %gain_ref.5, bf16[2,192,576]{2,1,0:T(8,128)(2,1)} %w_ref.5, bf16[2,192,192]{2,1,0:T(8,128)(2,1)} %p_ref.5, bf16[4,6,512,512]{3,2,1,0:T(8,128)(2,1)} %get-tuple-element.21.e_ref, ...), custom_call_target="tpu_custom_call" | custom-call | tf_op jit(solution)/shard_map/pallas_call | solution.py:230
  120.8 0.0 copy-done.1
  120.8 2.4 pad_maximum_fusion
  123.2 0.0 copy-start.2
  123.2 0.0 copy-start.3
  123.2 0.0 all-reduce.2.cloned.1.call-update
  123.2 0.7 copy-done.2
  123.9 0.0 copy-done.3
  123.9 66.0 %psum.14 = f32[2,192]{1,0:T(2,128)S(1)} all-reduce(f32[2,192]{1,0:T(2,128)S(1)} %maximum_reduce_fusion), channel_id=1, replica_groups=mesh['gy'=16,'gx'=8] {'gy','gx'}, use_global_device_ids=true, to_apply=%region_1.0 | all-reduce | flops 384 | bytes 3072 | tf_op jit(solution)/shard_map/psum | solution.py:303
  189.9 0.6 broadcast_multiply_fusion
  190.5 82.6 %all-reduce.2.cloned.1.call-done = f32[2,768,192]{2,1,0:T(8,128)} async-done(((f32[2,768,192]{2,1,0:T(8,128)}), f32[2,768,192]{2,1,0:T(8,128)}) %all-reduce.2.cloned.1.call-update) | async-done | bytes 1179664 | tf_op jit(solution)/shard_map/psum | solution.py:303
  273.0 1.3 fusion
  274.4 1.3 copy.10
  275.7 1.8 slice_multiply_fusion.1
  (4 shorter events, 0.1 us)
Async XLA Ops:
  7.2 1.2 copy-start
  7.2 265.8 %all-reduce.2.cloned.1.call-start = ((), (), s32[]{:S(2)}) async-start(), calls=%async_computation | async-start | bytes 3145728 | tf_op jit(solution)/shard_map/psum | solution.py:303
  8.6 27.2 %collective-permute-start.2 = (bf16[4,8,32,192]{3,2,1,0:T(8,128)(2,1)S(1)}, bf16[4,8,32,192]{3,2,1,0:T(8,128)(2,1)S(1)}, u32[]{:S(2)}, u32[]{:S(2)}) collective-permute-start(bf16[4,8,32,192]{3,2,1,0:T(8,128)(2,1)S(1)} %get-tuple-element.40), channel_id=1, source_target_pairs={{0,120},{8,0},{16,8},{24,16},{32,24},{40,32},{48,40},{56,48},{64,5... | collective-permute-start | bytes 1179656 | tf_op jit(solution)/shard_map/ppermute | solution.py:242
  32.5 9.6 %collective-permute-start = (bf16[4,8,32,192]{3,2,1,0:T(8,128)(2,1)S(1)}, bf16[4,8,32,192]{3,2,1,0:T(8,128)(2,1)S(1)}, u32[]{:S(2)}, u32[]{:S(2)}) collective-permute-start(bf16[4,8,32,192]{3,2,1,0:T(8,128)(2,1)S(1)} %get-tuple-element.42), channel_id=1, source_target_pairs={{0,120},{8,0},{16,8},{24,16},{32,24},{40,32},{48,40},{56,48},{64,5... | collective-permute-start | bytes 1179656 | tf_op jit(solution)/shard_map/ppermute | solution.py:242
  35.9 11.9 %collective-permute-start.3 = (bf16[1,8,64,192]{3,2,1,0:T(8,128)(2,1)S(1)}, bf16[1,8,64,192]{3,2,1,0:T(8,128)(2,1)S(1)}, u32[]{:S(2)}, u32[]{:S(2)}) collective-permute-start(bf16[1,8,64,192]{3,2,1,0:T(8,128)(2,1)S(1)} %pad_maximum_fusion.4), channel_id=1, source_target_pairs={{0,7},{1,0},{2,1},{3,2},{4,3},{5,4},{6,5},{7,6},{8,15},{9,8},{10,9... | collective-permute-start | bytes 589832 | tf_op jit(solution)/shard_map/ppermute | solution.py:242
  42.1 9.5 %collective-permute-start.1 = (bf16[1,8,64,192]{3,2,1,0:T(8,128)(2,1)S(1)}, bf16[1,8,64,192]{3,2,1,0:T(8,128)(2,1)S(1)}, u32[]{:S(2)}, u32[]{:S(2)}) collective-permute-start(bf16[1,8,64,192]{3,2,1,0:T(8,128)(2,1)S(1)} %pad_maximum_fusion.5), channel_id=1, source_target_pairs={{0,7},{1,0},{2,1},{3,2},{4,3},{5,4},{6,5},{7,6},{8,15},{9,8},{10,9... | collective-permute-start | bytes 589832 | tf_op jit(solution)/shard_map/ppermute | solution.py:242
  73.2 8.0 %collective-permute-start.4 = (bf16[4,8,32,192]{3,2,1,0:T(8,128)(2,1)S(1)}, bf16[4,8,32,192]{3,2,1,0:T(8,128)(2,1)S(1)}, u32[]{:S(2)}, u32[]{:S(2)}) collective-permute-start(bf16[4,8,32,192]{3,2,1,0:T(8,128)(2,1)S(1)} %get-tuple-element.38), channel_id=1, source_target_pairs={{0,8},{8,16},{16,24},{24,32},{32,40},{40,48},{48,56},{56,64},{64,7... | collective-permute-start | bytes 1179656 | tf_op jit(solution)/shard_map/ppermute | solution.py:242
  81.3 13.2 %collective-permute-start.5 = (bf16[1,8,64,192]{3,2,1,0:T(8,128)(2,1)S(1)}, bf16[1,8,64,192]{3,2,1,0:T(8,128)(2,1)S(1)}, u32[]{:S(2)}, u32[]{:S(2)}) collective-permute-start(bf16[1,8,64,192]{3,2,1,0:T(8,128)(2,1)S(1)} %pad_maximum_fusion.3), channel_id=1, source_target_pairs={{0,1},{1,2},{2,3},{3,4},{4,5},{5,6},{6,7},{7,0},{8,9},{9,10},{10,1... | collective-permute-start | bytes 589832 | tf_op jit(solution)/shard_map/ppermute | solution.py:242
  95.9 24.9 %copy-start.1 = (f32[768,192]{1,0:T(8,128)S(1)}, f32[768,192]{1,0:T(8,128)}, u32[]{:S(2)}) copy-start(f32[768,192]{1,0:T(8,128)} %get-tuple-element.33) | copy-start | bytes 1769476
  123.2 0.7 copy-start.2
  123.2 0.7 copy-start.3
Sparse Core Ops, SparseCore 0:
  123.3 149.6 all-reduce.1

commit v2 on v1

v2 whole, which is shorter than its diff:
```python
import functools
import math

import jax
import jax.numpy as jnp
from jax import lax
from jax.experimental import pallas as pl
from jax.experimental.pallas import tpu as pltpu
from jax.sharding import PartitionSpec as P

HEADS = 6
WIN = 8
C = 192
HD = 32
TOK = WIN**3
HALF = TOK // 2
EPSILON = 1e-05
MASKED = -1e30
SCALE = HD**-0.5
LOG2E = 1.0 / math.log(2.0)
LN2 = math.log(2.0)
F32 = jnp.float32
BF16 = jnp.bfloat16
GROUPS = ((0, 1, 2), (3, 4, 5))


def dot(left, right):
    return jnp.dot(left, right, preferred_element_type=F32)


def dot_t(left, right):
    return lax.dot_general(left, right, (((1,), (1,)), ((), ())), preferred_element_type=F32)


def rows(head, part=0):
    start = part * C + head * HD
    return slice(start, start + HD)


def layer_norm(x, gain_row):
    center = x - jnp.sum(x, axis=-1, keepdims=True) * (1.0 / C)
    inverse = lax.rsqrt(jnp.sum(center * center, axis=-1, keepdims=True) * (1.0 / C) + EPSILON)
    normed = center * inverse
    return (normed * gain_row).astype(BF16), normed, inverse


def norm_back(d_normed, normed, inverse, gain_row):
    scaled = d_normed * gain_row
    first = jnp.sum(scaled, axis=-1, keepdims=True) * (1.0 / C)
    second = jnp.sum(scaled * normed, axis=-1, keepdims=True) * (1.0 / C)
    return inverse * (scaled - first - normed * second)


def fold_tokens(x):
    return jnp.sum(x.reshape(TOK // 8, 8, C), axis=0)


def halves(first, second):
    a = first.astype(F32).reshape(TOK // 8, 8, C)
    b = second.astype(F32).reshape(TOK // 8, 8, C)
    place = lax.broadcasted_iota(jnp.int32, (TOK // 8, 8, C), 1)
    return jnp.where(place < 4, a, b).reshape(TOK, C)


def prepare_weights(block, w_ref, p_ref, wt_ref, wkv_ref, pt_ref):
    weight = w_ref[block].astype(F32)
    wt_ref[...] = weight.T.astype(BF16)
    wkv_ref[...] = weight[:, C:].astype(BF16)
    if pt_ref is not None:
        pt_ref[...] = p_ref[block].astype(F32).T.astype(BF16)


def project(normed_b, wt_ref, wkv_ref, qkvt_ref, kv_ref):
    qkvt_ref[:C] = (dot_t(wt_ref[:C], normed_b) * (SCALE * LOG2E)).astype(BF16)
    qkvt_ref[C:] = dot_t(wt_ref[C:], normed_b).astype(BF16)
    kv_ref[...] = dot(normed_b, wkv_ref[...]).astype(BF16)


def regular_forward(group, qkvt_ref, kv_ref, e_ref, r_ref, o_ref):
    s = [dot(kv_ref[:, rows(h)], qkvt_ref[rows(h)]) for h in group]
    m = [jnp.max(x, axis=0, keepdims=True) for x in s]
    ef = [jnp.exp2(x - y) for x, y in zip(s, m)]
    e = [x.astype(BF16) for x in ef]
    for h, x in zip(group, e):
        e_ref[h] = x
    r = [1.0 / jnp.sum(x, axis=0, keepdims=True) for x in ef]
    o = [dot(qkvt_ref[rows(h, 2)], x) for h, x in zip(group, e)]
    for h, x, y in zip(group, o, r):
        o_ref[rows(h)] = x * y
        r_ref[h : h + 1] = y


def regular_backward(group, qkvt_ref, kv_ref, e_ref, r_ref, o_ref, da_ref, dqkvt_ref):
    da = [(da_ref[rows(h)] * r_ref[h : h + 1]).astype(BF16) for h in group]
    d = [
        jnp.sum(x.astype(F32) * o_ref[rows(h)], axis=0, keepdims=True) for h, x in zip(group, da)
    ]
    dp = [dot(kv_ref[:, rows(h, 1)], x) for h, x in zip(group, da)]
    for h, x in zip(group, da):
        dqkvt_ref[rows(h, 2)] = dot_t(x, e_ref[h]).astype(BF16)
    ds = [
        (e_ref[h].astype(F32) * (x - y)).astype(BF16) for h, x, y in zip(group, dp, d)
    ]
    for h, x in zip(group, ds):
        dqkvt_ref[rows(h)] = (dot(qkvt_ref[rows(h, 1)], x) * SCALE).astype(BF16)
        dqkvt_ref[rows(h, 1)] = (dot_t(qkvt_ref[rows(h)], x) * LN2).astype(BF16)


def shifted_both(group, qkvt_ref, kv_ref, bias, o_ref, da_ref, dqkvt_ref):
    parts = [(h, slice(k * HALF, (k + 1) * HALF)) for h in group for k in range(2)]
    s = [dot(kv_ref[t, rows(h)], qkvt_ref[rows(h), t]) + bias for h, t in parts]
    m = [jnp.max(x, axis=0, keepdims=True) for x in s]
    ef = [jnp.exp2(x - y) for x, y in zip(s, m)]
    e = [x.astype(BF16) for x in ef]
    r = [1.0 / jnp.sum(x, axis=0, keepdims=True) for x in ef]
    o = [dot(qkvt_ref[rows(h, 2), t], x) * y for (h, t), x, y in zip(parts, e, r)]
    da = [(da_ref[rows(h), t] * y).astype(BF16) for (h, t), y in zip(parts, r)]
    d = [jnp.sum(x.astype(F32) * y, axis=0, keepdims=True) for x, y in zip(da, o)]
    dp = [dot(kv_ref[t, rows(h, 1)], x) for (h, t), x in zip(parts, da)]
    for (h, t), x, y, z in zip(parts, o, da, e):
        o_ref[rows(h), t] = x.astype(BF16)
        dqkvt_ref[rows(h, 2), t] = dot_t(y, z).astype(BF16)
    ds = [(x.astype(F32) * (y - z)).astype(BF16) for x, y, z in zip(e, dp, d)]
    for (h, t), x in zip(parts, ds):
        dqkvt_ref[rows(h), t] = (dot(qkvt_ref[rows(h, 1), t], x) * SCALE).astype(BF16)
        dqkvt_ref[rows(h, 1), t] = (dot_t(qkvt_ref[rows(h), t], x) * LN2).astype(BF16)


def write_bias(bias_ref):
    last_row = lax.axis_index("gy") == lax.axis_size("gy") - 1
    last_col = lax.axis_index("gx") == lax.axis_size("gx") - 1
    key = lax.broadcasted_iota(jnp.int32, (HALF, HALF), 0)
    query = lax.broadcasted_iota(jnp.int32, (HALF, HALF), 1)
    row_bias = jnp.where((key // 32) % 2 != (query // 32) % 2, MASKED, 0.0).astype(F32)
    col_bias = jnp.where((key // 4) % 2 != (query // 4) % 2, MASKED, 0.0).astype(F32)
    row_bias = row_bias * jnp.where(last_row, 1.0, 0.0).astype(F32)
    col_bias = col_bias * jnp.where(last_col, 1.0, 0.0).astype(F32)
    bias_ref[0] = row_bias
    bias_ref[1] = jnp.minimum(row_bias, col_bias)


def remote(src, dst, send, recv, target):
    return pltpu.make_async_remote_copy(
        src_ref=src,
        dst_ref=dst,
        send_sem=send,
        recv_sem=recv,
        device_id=target,
        device_id_type=pl.DeviceIdType.MESH,
    )


def loop(first, last, body):
    def step(i, carry):
        body(i)
        return carry

    lax.fori_loop(first, last, step, 0)


class Place:
    def __init__(self):
        self.ny, self.nx = lax.axis_size("gy"), lax.axis_size("gx")
        self.y, self.x = lax.axis_index("gy"), lax.axis_index("gx")

    def at(self, dy, dx):
        return (lax.rem(self.y + dy + self.ny, self.ny), lax.rem(self.x + dx + self.nx, self.nx))


def greet(place):
    barrier = pltpu.get_barrier_semaphore()

    def signal(target):
        pl.semaphore_signal(barrier, 1, device_id=target, device_id_type=pl.DeviceIdType.MESH)

    loop(1, place.ny, lambda i: signal(place.at(i, 0)))
    loop(1, place.nx, lambda i: signal(place.at(0, i)))
    signal(place.at(1, 1))
    signal(place.at(-1, -1))
    pl.semaphore_wait(barrier, place.ny + place.nx)


class Halo:
    def __init__(self, place, step, own, grid, send, recv):
        self.place, self.step, self.own, self.grid = place, step, own, grid
        self.send, self.recv = send, recv
        self.edge, self.into, self.base = (0, 4, 0) if step < 0 else (3, 0, 1)

    def row(self, w):
        return remote(
            self.own.at[w, :, 0:32],
            self.grid.at[w + self.base, :, 0:32],
            self.send.at[w],
            self.recv.at[w],
            self.place.at(self.step, 0),
        )

    def column(self):
        return remote(
            self.own.at[self.edge, :, 32:64],
            self.grid.at[self.into, :, 32:64],
            self.send.at[4],
            self.recv.at[4],
            self.place.at(0, self.step),
        )

    def corner(self):
        return remote(
            self.own.at[self.edge, :, 0:32],
            self.grid.at[self.into, :, 0:32],
            self.send.at[5],
            self.recv.at[5],
            self.place.at(self.step, self.step),
        )

    def start(self, w, values):
        self.own[w] = values
        self.grid[w + self.base, :, 32:64] = values[:, 32:64]
        self.row(w).start()

        @pl.when(w == self.edge)
        def _():
            self.column().start()
            self.corner().start()

    def arrived(self, w):
        self.row(w).wait_recv()

    def edge_arrived(self):
        self.column().wait_recv()
        self.corner().wait_recv()

    def finish(self):
        loop(0, 4, lambda w: self.row(w).wait_send())
        self.column().wait_send()
        self.corner().wait_send()


class Reduce:
    def __init__(self, place, total, chunks, part, mid, full, sems):
        self.place, self.total, self.chunks = place, total, chunks
        self.part, self.mid, self.full = part, mid, full
        self.s1, self.r1, self.s2, self.r2, self.s3, self.r3 = sems

    def scatter(self, i):
        to = self.place.at(i, 0)
        return remote(
            self.chunks.at[to[0]], self.part.at[i - 1], self.s1.at[i - 1], self.r1.at[i - 1], to
        )

    def across(self, i):
        mine = self.mid.at[self.place.x]
        return remote(mine, mine, self.s2.at[i - 1], self.r2.at[self.place.x], self.place.at(0, i))

    def gather(self, i):
        mine = self.full.at[self.place.y]
        return remote(mine, mine, self.s3.at[i - 1], self.r3.at[self.place.y], self.place.at(i, 0))

    def start(self, gsum):
        gain = jnp.sum(gsum, axis=0, keepdims=True)
        first = lax.broadcasted_iota(jnp.int32, (8, 64), 0) == 0
        self.total[:, C:] = jnp.zeros((self.total.shape[0], 64), F32)
        for k in range(3):
            piece = jnp.broadcast_to(gain[:, 64 * k : 64 * k + 64], (8, 64))
            self.total[8 * k : 8 * k + 8, C:] = jnp.where(first, piece, 0.0)
        self.chunks[...] = self.total[...].astype(BF16).reshape(self.chunks.shape)
        loop(1, self.place.ny, lambda i: self.scatter(i).start())

    def middle(self):
        loop(1, self.place.ny, lambda i: self.scatter(i).wait_recv())
        size = self.chunks.shape[1]
        acc = self.total[pl.ds(pl.multiple_of(self.place.y * size, 16), size)]
        for i in range(self.place.ny - 1):
            acc += self.part[i].astype(F32)
        self.mid[self.place.x] = acc.astype(BF16)
        loop(1, self.place.nx, lambda i: self.across(i).start())

    def spread(self, factor):
        def arrived(i):
            x = self.place.at(0, i)[1]
            remote(
                self.mid.at[x], self.mid.at[x], self.s2.at[i - 1], self.r2.at[x], self.place.at(0, i)
            ).wait_recv()

        loop(1, self.place.nx, arrived)
        acc = self.mid[0].astype(F32)
        for i in range(1, self.place.nx):
            acc += self.mid[i].astype(F32)
        self.full[self.place.y] = (acc * factor).astype(BF16)
        loop(1, self.place.ny, lambda i: self.gather(i).start())

    def finish(self, block, gain_ref, qkv_ref, proj_ref):
        def arrived(i):
            y = self.place.at(i, 0)[0]
            remote(
                self.full.at[y], self.full.at[y], self.s3.at[i - 1], self.r3.at[y], self.place.at(i, 0)
            ).wait_recv()

        loop(1, self.place.ny, arrived)
        whole = self.full[...].reshape(self.total.shape).astype(F32)
        qkv_ref[block] = whole[: 3 * C, :C].T
        proj_ref[block] = whole[3 * C :, :C]
        for k in range(3):
            gain_ref[block : block + 1, 64 * k : 64 * k + 64] = whole[8 * k : 8 * k + 1, C:]

    def drain(self):
        loop(1, self.place.ny, lambda i: self.scatter(i).wait_send())
        loop(1, self.place.nx, lambda i: self.across(i).wait_send())
        loop(1, self.place.ny, lambda i: self.gather(i).wait_send())


def kernel(
    factor,
    tok_ref, cot_ref, gain_ref, w_ref, p_ref,
    out_ref, ggain_ref, gqkv_ref, gproj_ref,
    x32_ref, wt_ref, wkv_ref, pt_ref, bias_ref,
    e_ref, r_ref, o_ref, qkvt_ref, kv_ref, nb_ref, normed_ref, inv_ref,
    qkvt1_ref, kv1_ref, o1_ref, da_ref, dqkvt_ref, total_ref, gsum_ref,
    own_ref, grid_ref, chunks_ref, part_ref, mid_ref, full_ref,
    hsend, hrecv, s1, r1, s2, r2, s3, r3,
):
    place = Place()
    greet(place)
    cot, middle, back = (
        Halo(place, step, own_ref.at[k], grid_ref.at[k], hsend.at[k], hrecv.at[k])
        for k, step in enumerate((-1, -1, 1))
    )
    sums = [
        Reduce(
            place, total_ref.at[k], chunks_ref.at[k], part_ref.at[k], mid_ref.at[k], full_ref.at[k],
            [s.at[k] for s in (s1, r1, s2, r2, s3, r3)],
        )
        for k in range(2)
    ]

    def columns(w):
        return pl.ds(pl.multiple_of(w * WIN, WIN), WIN)

    x32_ref[...] = cot_ref[...].astype(F32)

    def send_cotangent(w):
        cot.start(w, x32_ref[:, :, columns(w), :].reshape(TOK, C).astype(BF16).reshape(WIN, 64, C))

    loop(0, 4, send_cotangent)

    x32_ref[...] = tok_ref[...].astype(F32)
    for block in range(2):
        prepare_weights(
            block, w_ref, p_ref, wt_ref.at[block], wkv_ref.at[block], None if block else pt_ref
        )
    write_bias(bias_ref)
    total_ref[...] = jnp.zeros_like(total_ref)
    gsum_ref[...] = jnp.zeros_like(gsum_ref)

    def regular_window(w):
        x = x32_ref[:, :, columns(w), :].reshape(TOK, C)
        normed_b, normed, inverse = layer_norm(x, gain_ref[0:1])
        nb_ref[w] = normed_b
        normed_ref[w] = normed
        inv_ref[w] = inverse
        project(normed_b, wt_ref.at[0], wkv_ref.at[0], qkvt_ref.at[w], kv_ref.at[w])
        for group in GROUPS:
            regular_forward(
                group, qkvt_ref.at[w], kv_ref.at[w], e_ref.at[w], r_ref.at[w], o_ref.at[w]
            )
        branch = dot(pt_ref[...], o_ref[w].astype(BF16)).T
        middle.start(w, (x + branch).astype(BF16).reshape(WIN, 64, C))

    loop(0, 4, regular_window)

    loop(0, 4, cot.arrived)
    cot.edge_arrived()
    middle.arrived(0)

    def shifted_window(w):
        @pl.when(w < 3)
        def _():
            middle.arrived(w + 1)

        @pl.when(w == 3)
        def _():
            middle.edge_arrived()

        x = halves(middle.grid[w + 1].reshape(TOK, C), middle.grid[w].reshape(TOK, C))
        normed_b, normed, inverse = layer_norm(x, gain_ref[1:2])
        project(normed_b, wt_ref.at[1], wkv_ref.at[1], qkvt1_ref, kv1_ref)
        g = halves(cot.grid[w + 1].reshape(TOK, C), cot.grid[w].reshape(TOK, C))
        g_b = g.astype(BF16)
        da_ref[...] = dot_t(p_ref[1], g_b)
        bias = bias_ref[w // 3]
        for group in GROUPS:
            shifted_both(group, qkvt1_ref, kv1_ref, bias, o1_ref, da_ref, dqkvt_ref)
        total_ref[1, 3 * C :, :C] += dot(o1_ref[...], g_b)
        total_ref[1, : 3 * C, :C] += dot(dqkvt_ref[...], normed_b)
        d_normed = dot(w_ref[1], dqkvt_ref[...]).T
        gsum_ref[1] += fold_tokens(d_normed * normed)
        grad = g + norm_back(d_normed, normed, inverse, gain_ref[1:2])
        back.start(w, grad.astype(BF16).reshape(WIN, 64, C))

    loop(0, 4, shifted_window)
    sums[1].start(gsum_ref[1])
    back.arrived(0)

    def backward_window(t):
        w = lax.rem(t + 1, 4)

        @pl.when(t < 3)
        def _():
            back.arrived(t + 1)

        @pl.when(t == 3)
        def _():
            back.edge_arrived()

        @pl.when(t == 1)
        def _():
            sums[1].middle()

        @pl.when(t == 2)
        def _():
            sums[1].spread(factor)

        g = halves(back.grid[w].reshape(TOK, C), back.grid[w + 1].reshape(TOK, C))
        g_b = g.astype(BF16)
        da_ref[...] = dot_t(p_ref[0], g_b)
        for group in GROUPS:
            regular_backward(
                group, qkvt_ref.at[w], kv_ref.at[w], e_ref.at[w], r_ref.at[w], o_ref.at[w],
                da_ref, dqkvt_ref,
            )
        total_ref[0, 3 * C :, :C] += dot(o_ref[w].astype(BF16), g_b)
        total_ref[0, : 3 * C, :C] += dot(dqkvt_ref[...], nb_ref[w])
        d_normed = dot(w_ref[0], dqkvt_ref[...]).T
        normed = normed_ref[w]
        gsum_ref[0] += fold_tokens(d_normed * normed)
        out = g + norm_back(d_normed, normed, inv_ref[w], gain_ref[0:1])
        out_ref[:, :, columns(w), :] = out.reshape(WIN, WIN, WIN, C)

    loop(0, 4, backward_window)
    sums[0].start(gsum_ref[0])
    sums[1].finish(1, ggain_ref, gqkv_ref, gproj_ref)
    sums[0].middle()
    for halo in (cot, middle, back):
        halo.finish()
    sums[1].drain()
    sums[0].spread(factor)
    sums[0].finish(0, ggain_ref, gqkv_ref, gproj_ref)
    sums[0].drain()


def local(tokens, cotangent, gains, qkv_weight, proj_weight):
    depth_count, row_count, col_count, features = tokens.shape
    ny, nx = lax.axis_size("gy"), lax.axis_size("gx")
    factor = (depth_count * row_count * col_count * ny * nx // 16) ** (-0.5)
    size = 4 * C // ny
    whole = pl.BlockSpec(memory_space=pltpu.VMEM)
    outs = [((WIN, WIN, 32, C), F32), ((2, C), F32), ((2, C, 3 * C), F32), ((2, C, C), F32)]
    scratch = [
        ((WIN, WIN, 32, C), F32),
        ((2, 3 * C, C), BF16),
        ((2, C, 2 * C), BF16),
        ((C, C), BF16),
        ((2, HALF, HALF), F32),
        ((4, HEADS, TOK, TOK), BF16),
        ((4, 8, TOK), F32),
        ((4, C, TOK), F32),
        ((4, 3 * C, TOK), BF16),
        ((4, TOK, 2 * C), BF16),
        ((4, TOK, C), BF16),
        ((4, TOK, C), F32),
        ((4, TOK, 1), F32),
        ((3 * C, TOK), BF16),
        ((TOK, 2 * C), BF16),
        ((C, TOK), BF16),
        ((C, TOK), F32),
        ((3 * C, TOK), BF16),
        ((2, 4 * C, 256), F32),
        ((2, 8, C), F32),
        ((3, 4, WIN, 64, C), BF16),
        ((3, 5, WIN, 64, C), BF16),
        ((2, ny, size, 256), BF16),
        ((2, ny - 1, size, 256), BF16),
        ((2, nx, size, 256), BF16),
        ((2, ny, size, 256), BF16),
    ]
    sems = [(3, 6), (3, 6), (2, ny), (2, ny), (2, nx), (2, nx), (2, ny), (2, ny)]
    return pl.pallas_call(
        functools.partial(kernel, factor),
        out_shape=[jax.ShapeDtypeStruct(*o) for o in outs],
        in_specs=[whole] * 5,
        out_specs=[whole] * 4,
        scratch_shapes=[pltpu.VMEM(*s) for s in scratch]
        + [pltpu.SemaphoreType.DMA(s) for s in sems],
        compiler_params=pltpu.CompilerParams(
            vmem_limit_bytes=60 * 2**20, collective_id=0, has_side_effects=True
        ),
    )(tokens, cotangent, gains, qkv_weight, proj_weight)


def solution(mesh):
    in_specs = (P(None, "gy", "gx", None), P(None, "gy", "gx", None), P(), P(), P())
    out_specs = (P(None, "gy", "gx", None), P(), P(), P())
    return jax.shard_map(local, mesh=mesh, in_specs=in_specs, out_specs=out_specs, check_vma=False)
```

time: 285 us -> 93.6 us (0.33)
  waiting for transfers between devices: 103 us -> 0 us
  blocking collectives: 66 us -> 0 us
  Pallas kernels: 65 us -> 87.2 us
  starting transfers between devices: 20 us -> 0 us
  between operations: 14.1 us -> 0.67 us
  other arithmetic: 10.3 us -> 0 us
    psum x1 -> x0, waiting for transfers between devices: 82.6 us -> none  [local(): lax.psum((jnp.stack([wsum_zero, wsum_one]), jnp.stack([gsum_zero, gsum_on...]
    psum x1 -> x0, blocking collectives: 66 us -> none  [local(): lax.psum((jnp.stack([wsum_zero, wsum_one]), jnp.stack([gsum_zero, gsum_on...]
    pallas_call x3 -> x1, Pallas kernels: 65 us -> 87.2 us  [local(): pl.pallas_call(functools.partial(kernel, factor), out_shape=[jax.ShapeDty...]
    ppermute x6 -> x0, waiting for transfers between devices: 20.4 us -> none  [pass_along(): lax.ppermute(value, axis, [(i, (i + steps) % count) for i in range(count)])]
    ppermute x6 -> x0, starting transfers between devices: 19.9 us -> none  [pass_along(): lax.ppermute(value, axis, [(i, (i + steps) % count) for i in range(count)])]
    concatenate x6 -> x0, other arithmetic: 4.22 us -> none  [the longest x2 2.72 us: pull_ahead(): return jnp.concatenate([ahead, pass_along(ahead[:1], 'gx', -1)], axis=0)]
    mul x3 -> x0, other arithmetic: 3.7 us -> none  [the longest x1 1.77 us: local(): wsum[:, 3 * C:] * factor]
  transfers between devices with their start and end apart: 7 -> 0, of which waited for: 4 -> 0; matrix products, arithmetic and copies ran while one was open for 1% -> 0% of each run, Pallas kernels for 7% -> 0%
where the time goes in v2:
time: 93.6 us; the launch traced here: 93.5 us
  Pallas kernels  87.2 us (93%)
  local copies, waits for them, and re-layouts  5.54 us (6%)
    pallas_call x1, Pallas kernels, local(): pl.pallas_call(functools.partial(kernel, factor), out_shape=[jax.ShapeDty...  87.2 us
    unnamed x10, local copies, waits for them, and re-layouts  5.54 us

profile of v2, /device:TPU:1, one launch (start us, length us, event | category | flops | bytes accessed | tf_op | source)
XLA Modules:
  0.0 93.5 jit_solution(8585532793014704595)
XLA Ops:
  0.6 87.2 %shard_map.84 = (f32[8,8,32,192]{3,2,1,0:T(8,128)}, f32[2,192]{1,0:T(2,128)}, f32[2,192,576]{2,1,0:T(8,128)}, f32[2,192,192]{2,1,0:T(8,128)}) custom-call(bf16[8,8,32,192]{3,2,1,0:T(8,128)(2,1)} %tok_ref.1, bf16[8,8,32,192]{3,2,1,0:T(8,128)(2,1)} %cot_ref.1, f32[2,192]{1,0:T(2,128)} %gain_ref.1, bf16[2,192,576]{2,1,0:T(8,128)(2,1)} %w_ref.1, ...), custom_call_target="tpu_custom_call" | custom-call | tf_op jit(solution)/shard_map/pallas_call | solution.py:487
  87.9 0.0 copy-start.2
  87.9 0.0 copy-start
  87.9 0.0 copy-start.1
  87.9 3.3 %copy.13 = f32[8,8,32,192]{3,2,1,0:T(8,128)} copy(f32[8,8,32,192]{3,2,1,0:T(8,128)} %get-tuple-element.8) | data formatting | bytes 3145728
  91.2 0.0 copy-done.2
  91.2 0.6 copy.14
  91.8 0.0 copy-done
  91.8 0.9 %copy.15 = f32[2,192,576]{2,1,0:T(8,128)} copy(f32[2,192,576]{2,1,0:T(8,128)S(1)} %copy-done) | data formatting | bytes 1769472
  92.7 0.0 copy-done.1
  92.7 0.7 copy.16
Async XLA Ops:
  87.9 3.3 %copy-start.2 = (f32[2,192]{1,0:T(2,128)S(1)}, f32[2,192]{1,0:T(2,128)}, u32[]{:S(2)}) copy-start(f32[2,192]{1,0:T(2,128)} %get-tuple-element.9) | copy-start | bytes 4612
  87.9 3.9 %copy-start = (f32[2,192,576]{2,1,0:T(8,128)S(1)}, f32[2,192,576]{2,1,0:T(8,128)}, u32[]{:S(2)}) copy-start(f32[2,192,576]{2,1,0:T(8,128)} %get-tuple-element.10) | copy-start | bytes 2654212
  87.9 4.8 %copy-start.1 = (f32[2,192,192]{2,1,0:T(8,128)S(1)}, f32[2,192,192]{2,1,0:T(8,128)}, u32[]{:S(2)}) copy-start(f32[2,192,192]{2,1,0:T(8,128)} %get-tuple-element.11) | copy-start | bytes 884740

commit v3 on v2

v3 whole, which is shorter than its diff:
```python
import functools
import math

import jax
import jax.numpy as jnp
from jax import lax
from jax.experimental import pallas as pl
from jax.experimental.pallas import tpu as pltpu
from jax.sharding import PartitionSpec as P

HEADS = 6
WIN = 8
C = 192
HD = 32
TOK = WIN**3
HALF = TOK // 2
EPSILON = 1e-05
MASKED = -1e30
SCALE = HD**-0.5
LOG2E = 1.0 / math.log(2.0)
LN2 = math.log(2.0)
F32 = jnp.float32
BF16 = jnp.bfloat16
GROUPS = ((0, 1, 2), (3, 4, 5))
FIRST = 384
PIECES = ((0, 512), (512, 768))


def dot(left, right):
    return jnp.dot(left, right, preferred_element_type=F32)


def dot_t(left, right):
    return lax.dot_general(left, right, (((1,), (1,)), ((), ())), preferred_element_type=F32)


def rows(head, part=0):
    start = part * 128 + head * HD if head < 4 else FIRST + part * 64 + (head - 4) * HD
    return slice(start, start + HD)


def own_rows(head):
    return slice(head * HD, head * HD + HD)


def columns_of(head, part):
    start = part * 128 + head * HD if head < 4 else 256 + part * 64 + (head - 4) * HD
    return slice(start, start + HD)


def layer_norm(x, gain_row):
    center = x - jnp.sum(x, axis=-1, keepdims=True) * (1.0 / C)
    inverse = lax.rsqrt(jnp.sum(center * center, axis=-1, keepdims=True) * (1.0 / C) + EPSILON)
    normed = center * inverse
    return (normed * gain_row).astype(BF16), normed, inverse


def norm_back(d_normed, normed, inverse, gain_row):
    scaled = d_normed * gain_row
    first = jnp.sum(scaled, axis=-1, keepdims=True) * (1.0 / C)
    second = jnp.sum(scaled * normed, axis=-1, keepdims=True) * (1.0 / C)
    return inverse * (scaled - first - normed * second)


def halves(first, second):
    a = first.astype(F32).reshape(TOK // 8, 8, C)
    b = second.astype(F32).reshape(TOK // 8, 8, C)
    place = lax.broadcasted_iota(jnp.int32, (TOK // 8, 8, C), 1)
    return jnp.where(place < 4, a, b).reshape(TOK, C)


def prepare_weights(block, w_ref, p_ref, wt_ref, wp_ref, wkv_ref, pt_ref):
    turned = w_ref[block].astype(F32).T
    starts = ((0, 128), (C, C + 128), (2 * C, 2 * C + 128), (128, C), (C + 128, 2 * C), (2 * C + 128, 3 * C))
    turned = jnp.concatenate([turned[a:b] for a, b in starts], axis=0)
    wt_ref[...] = turned.astype(BF16)
    wp_ref[...] = turned.T.astype(BF16)
    wkv_ref[...] = jnp.concatenate([turned[128:FIRST], turned[FIRST + 64 :]], axis=0).T.astype(BF16)
    if pt_ref is not None:
        pt_ref[...] = p_ref[block].astype(F32).T.astype(BF16)


def project(normed_b, wt_ref, wkv_ref, qkvt_ref, kv_ref):
    qkvt = dot_t(wt_ref[...], normed_b)
    qkvt_ref[:128] = (qkvt[:128] * (SCALE * LOG2E)).astype(BF16)
    qkvt_ref[128:FIRST] = qkvt[128:FIRST].astype(BF16)
    qkvt_ref[FIRST : FIRST + 64] = (qkvt[FIRST : FIRST + 64] * (SCALE * LOG2E)).astype(BF16)
    qkvt_ref[FIRST + 64 :] = qkvt[FIRST + 64 :].astype(BF16)
    kv_ref[...] = dot(normed_b, wkv_ref[...]).astype(BF16)


def regular_forward(group, qkvt_ref, kv_ref, e_ref, r_ref, o_ref):
    s = [dot(kv_ref[:, columns_of(h, 0)], qkvt_ref[rows(h)]) for h in group]
    m = [jnp.max(x, axis=0, keepdims=True) for x in s]
    ef = [jnp.exp2(x - y) for x, y in zip(s, m)]
    e = [x.astype(BF16) for x in ef]
    for h, x in zip(group, e):
        e_ref[h] = x
    r = [1.0 / jnp.sum(x, axis=0, keepdims=True) for x in ef]
    o = [dot(qkvt_ref[rows(h, 2)], x) for h, x in zip(group, e)]
    for h, x, y in zip(group, o, r):
        o_ref[own_rows(h)] = x * y
        r_ref[h : h + 1] = y


def regular_backward(group, qkvt_ref, kv_ref, e_ref, r_ref, o_ref, da_ref, dqkvt_ref):
    da = [(da_ref[own_rows(h)] * r_ref[h : h + 1]).astype(BF16) for h in group]
    d = [
        jnp.sum(x.astype(F32) * o_ref[own_rows(h)], axis=0, keepdims=True) for h, x in zip(group, da)
    ]
    dp = [dot(kv_ref[:, columns_of(h, 1)], x) for h, x in zip(group, da)]
    for h, x in zip(group, da):
        dqkvt_ref[rows(h, 2)] = dot_t(x, e_ref[h]).astype(BF16)
    ds = [
        (e_ref[h].astype(F32) * (x - y)).astype(BF16) for h, x, y in zip(group, dp, d)
    ]
    for h, x in zip(group, ds):
        dqkvt_ref[rows(h)] = (dot(qkvt_ref[rows(h, 1)], x) * SCALE).astype(BF16)
        dqkvt_ref[rows(h, 1)] = (dot_t(qkvt_ref[rows(h)], x) * LN2).astype(BF16)


def shifted_both(group, qkvt_ref, kv_ref, bias, o_ref, da_ref, dqkvt_ref):
    parts = [(h, slice(k * HALF, (k + 1) * HALF)) for h in group for k in range(2)]
    s = [dot(kv_ref[t, columns_of(h, 0)], qkvt_ref[rows(h), t]) + bias for h, t in parts]
    m = [jnp.max(x, axis=0, keepdims=True) for x in s]
    ef = [jnp.exp2(x - y) for x, y in zip(s, m)]
    e = [x.astype(BF16) for x in ef]
    r = [1.0 / jnp.sum(x, axis=0, keepdims=True) for x in ef]
    o = [dot(qkvt_ref[rows(h, 2), t], x) * y for (h, t), x, y in zip(parts, e, r)]
    da = [(da_ref[own_rows(h), t] * y).astype(BF16) for (h, t), y in zip(parts, r)]
    d = [jnp.sum(x.astype(F32) * y, axis=0, keepdims=True) for x, y in zip(da, o)]
    dp = [dot(kv_ref[t, columns_of(h, 1)], x) for (h, t), x in zip(parts, da)]
    for (h, t), x, y, z in zip(parts, o, da, e):
        o_ref[own_rows(h), t] = x.astype(BF16)
        dqkvt_ref[rows(h, 2), t] = dot_t(y, z).astype(BF16)
    ds = [(x.astype(F32) * (y - z)).astype(BF16) for x, y, z in zip(e, dp, d)]
    for (h, t), x in zip(parts, ds):
        dqkvt_ref[rows(h), t] = (dot(qkvt_ref[rows(h, 1), t], x) * SCALE).astype(BF16)
        dqkvt_ref[rows(h, 1), t] = (dot_t(qkvt_ref[rows(h), t], x) * LN2).astype(BF16)


def write_bias(bias_ref):
    last_row = lax.axis_index("gy") == lax.axis_size("gy") - 1
    last_col = lax.axis_index("gx") == lax.axis_size("gx") - 1
    key = lax.broadcasted_iota(jnp.int32, (HALF, HALF), 0)
    query = lax.broadcasted_iota(jnp.int32, (HALF, HALF), 1)
    row_bias = jnp.where((key // 32) % 2 != (query // 32) % 2, MASKED, 0.0).astype(F32)
    col_bias = jnp.where((key // 4) % 2 != (query // 4) % 2, MASKED, 0.0).astype(F32)
    row_bias = row_bias * jnp.where(last_row, 1.0, 0.0).astype(F32)
    col_bias = col_bias * jnp.where(last_col, 1.0, 0.0).astype(F32)
    bias_ref[0] = row_bias
    bias_ref[1] = jnp.minimum(row_bias, col_bias)


def remote(src, dst, send, recv, target):
    return pltpu.make_async_remote_copy(
        src_ref=src,
        dst_ref=dst,
        send_sem=send,
        recv_sem=recv,
        device_id=target,
        device_id_type=pl.DeviceIdType.MESH,
    )


def loop(first, last, body):
    def step(i, carry):
        body(i)
        return carry

    lax.fori_loop(first, last, step, 0)


def sizes_of(ny, nx):
    along_x = min(4, ny // 2)
    return along_x, ny // (2 * along_x), nx // 2


class Place:
    def __init__(self):
        self.ny, self.nx = lax.axis_size("gy"), lax.axis_size("gx")
        self.y, self.x = lax.axis_index("gy"), lax.axis_index("gx")
        self.nxx, self.nlow, self.nz = sizes_of(self.ny, self.nx)
        self.n1, self.n2 = self.nxx * self.nz, 4 * self.nlow
        core, across = lax.rem(self.y, 2), lax.rem(self.y // 2, self.nxx)
        low, z, high = self.y // (2 * self.nxx), self.x // 2, lax.rem(self.x, 2)
        self.core, self.low, self.high = core, low, high
        self.plane = across * self.nz + z
        self.across, self.z = across, z
        self.stack = (core * self.nlow + low) * 2 + high

    def at(self, dy, dx):
        return (lax.rem(self.y + dy + self.ny, self.ny), lax.rem(self.x + dx + self.nx, self.nx))

    def in_plane(self, i):
        k = lax.rem(self.plane + i, self.n1)
        across, z = k // self.nz, lax.rem(k, self.nz)
        return (self.low * (2 * self.nxx) + across * 2 + self.core, z * 2 + self.high), k

    def in_stack(self, i):
        k = lax.rem(self.stack + i, self.n2)
        core, low, high = k // (2 * self.nlow), lax.rem(k // 2, self.nlow), lax.rem(k, 2)
        return (low * (2 * self.nxx) + self.across * 2 + core, self.z * 2 + high), k


def greet(place):
    barrier = pltpu.get_barrier_semaphore()

    def signal(target):
        pl.semaphore_signal(barrier, 1, device_id=target, device_id_type=pl.DeviceIdType.MESH)

    loop(1, place.n1, lambda i: signal(place.in_plane(i)[0]))
    loop(1, place.n2, lambda i: signal(place.in_stack(i)[0]))
    for step in (-1, 1):
        signal(place.at(step, 0))
        signal(place.at(0, step))
        signal(place.at(step, step))
    return lambda: pl.semaphore_wait(barrier, place.n1 + place.n2 + 4)


def pack(window):
    pairs = window.astype(F32).reshape(32, 2, 8, C)
    place = lax.broadcasted_iota(jnp.int32, (32, 8, C), 1)
    packed = jnp.where(place < 4, pairs[:, 0], pltpu.roll(pairs[:, 1], 4, 1))
    return packed.astype(BF16).reshape(8, 32, C)


def unpack(packed):
    values = packed.astype(F32).reshape(32, 8, C)
    pairs = jnp.stack([values, pltpu.roll(values, 4, 1)], axis=1)
    return pairs.reshape(TOK, C).astype(BF16).reshape(8, 64, C)


class Halo:
    def __init__(self, place, step, own, grid, edge_own, edge_grid, send, recv):
        self.place, self.step, self.own, self.grid = place, step, own, grid
        self.edge_own, self.edge_grid = edge_own, edge_grid
        self.send, self.recv = send, recv
        self.edge, self.into, self.base = (0, 4, 0) if step < 0 else (3, 0, 1)

    def row(self, w):
        return remote(
            self.own.at[w, :, 0:32],
            self.grid.at[w + self.base, :, 0:32],
            self.send.at[w],
            self.recv.at[w],
            self.place.at(self.step, 0),
        )

    def column(self):
        return remote(
            self.edge_own.at[:, 16:32],
            self.edge_grid.at[:, 16:32],
            self.send.at[4],
            self.recv.at[4],
            self.place.at(0, self.step),
        )

    def corner(self):
        return remote(
            self.edge_own.at[:, 0:16],
            self.edge_grid.at[:, 0:16],
            self.send.at[5],
            self.recv.at[5],
            self.place.at(self.step, self.step),
        )

    def stage(self, w, values):
        self.own[w] = values
        self.grid[w + self.base, :, 32:64] = values[:, 32:64]

        @pl.when(w == self.edge)
        def _():
            self.edge_own[...] = pack(values)

    def start(self, w):
        self.row(w).start()

        @pl.when(w == self.edge)
        def _():
            self.column().start()
            self.corner().start()

    def arrived(self, w):
        self.row(w).wait_recv()

    def edge_arrived(self):
        self.column().wait_recv()
        self.corner().wait_recv()
        self.grid[self.into] = unpack(self.edge_grid[...])

    def finish(self):
        loop(0, 4, lambda w: self.row(w).wait_send())
        self.column().wait_send()
        self.corner().wait_send()


class Reduce:
    def __init__(self, place, total, chunks, part, mid, full, sems):
        self.place, self.total, self.chunks = place, total, chunks
        self.part, self.mid, self.full = part, mid, full
        self.s1, self.r1, self.s2, self.r2, self.s3, self.r3 = sems

    def scatter(self, i):
        to, k = self.place.in_plane(i)
        return remote(self.chunks.at[k], self.part.at[i - 1], self.s1.at[i - 1], self.r1.at[i - 1], to)

    def across(self, i):
        mine = self.mid.at[self.place.stack]
        to = self.place.in_stack(i)[0]
        return remote(mine, mine, self.s2.at[i - 1], self.r2.at[self.place.stack], to)

    def gather(self, i):
        mine = self.full.at[self.place.plane]
        to = self.place.in_plane(i)[0]
        return remote(mine, mine, self.s3.at[i - 1], self.r3.at[self.place.plane], to)

    def start(self):
        self.chunks[...] = self.total[...].astype(BF16).reshape(self.chunks.shape)
        loop(1, self.place.n1, lambda i: self.scatter(i).start())

    def middle(self):
        loop(1, self.place.n1, lambda i: self.scatter(i).wait_recv())
        size = self.chunks.shape[1]
        acc = self.total[pl.ds(pl.multiple_of(self.place.plane * size, 16), size)]
        for i in range(self.place.n1 - 1):
            acc += self.part[i].astype(F32)
        self.mid[self.place.stack] = acc.astype(BF16)
        loop(1, self.place.n2, lambda i: self.across(i).start())

    def spread(self, factor):
        def arrived(i):
            to, k = self.place.in_stack(i)
            remote(self.mid.at[k], self.mid.at[k], self.s2.at[i - 1], self.r2.at[k], to).wait_recv()

        loop(1, self.place.n2, arrived)
        acc = self.mid[0].astype(F32)
        for i in range(1, self.place.n2):
            acc += self.mid[i].astype(F32)
        self.full[self.place.plane] = (acc * factor).astype(BF16)
        loop(1, self.place.n1, lambda i: self.gather(i).start())

    def finish(self, result):
        def arrived(i):
            to, k = self.place.in_plane(i)
            remote(self.full.at[k], self.full.at[k], self.s3.at[i - 1], self.r3.at[k], to).wait_recv()

        loop(1, self.place.n1, arrived)
        result[...] = self.full[...].reshape(result.shape)

    def drain(self):
        loop(1, self.place.n1, lambda i: self.scatter(i).wait_send())
        loop(1, self.place.n2, lambda i: self.across(i).wait_send())
        loop(1, self.place.n1, lambda i: self.gather(i).wait_send())


def kernel(
    factor,
    tok_ref, cot_ref, gain_ref, w_ref, p_ref,
    out_ref, res1_ref, resa_ref, resb_ref,
    x32_ref, wt_ref, wp_ref, wkv_ref, pt_ref, bias_ref,
    e_ref, r_ref, o_ref, qkvt_ref, kv_ref, nb_ref, normed_ref, inv_ref,
    qkvt1_ref, kv1_ref, o1_ref, da_ref, dqkvt_ref, gb_ref, total_ref,
    own_ref, grid_ref, edge_own_ref, edge_grid_ref,
    ch1, pa1, mi1, fu1, cha, paa, mia, fua, chb, pab, mib, fub,
    hsend, hrecv, s1, r1, s2, r2, s3, r3, osem,
):
    place = Place()
    wait_for_peers = greet(place)
    cot, middle, back = (
        Halo(
            place, step, own_ref.at[k], grid_ref.at[k], edge_own_ref.at[k], edge_grid_ref.at[k],
            hsend.at[k], hrecv.at[k],
        )
        for k, step in enumerate((-1, -1, 1))
    )
    sum1, suma, sumb = (
        Reduce(place, total, *refs, [s.at[k] for s in (s1, r1, s2, r2, s3, r3)])
        for k, (total, refs) in enumerate(
            [
                (total_ref.at[1], (ch1, pa1, mi1, fu1)),
                (total_ref.at[0, slice(*PIECES[0])], (cha, paa, mia, fua)),
                (total_ref.at[0, slice(*PIECES[1])], (chb, pab, mib, fub)),
            ]
        )
    )

    def columns(w):
        return pl.ds(pl.multiple_of(w * WIN, WIN), WIN)

    x32_ref[...] = cot_ref[...].astype(F32)

    def stage_cotangent(w):
        cot.stage(w, x32_ref[:, :, columns(w), :].reshape(TOK, C).astype(BF16).reshape(WIN, 64, C))

    loop(0, 4, stage_cotangent)

    x32_ref[...] = tok_ref[...].astype(F32)
    for block in range(2):
        prepare_weights(
            block, w_ref, p_ref, wt_ref.at[block], wp_ref.at[block], wkv_ref.at[block],
            None if block else pt_ref,
        )
    write_bias(bias_ref)
    total_ref[...] = jnp.zeros_like(total_ref)

    def regular_window(w):
        x = x32_ref[:, :, columns(w), :].reshape(TOK, C)
        normed_b, normed, inverse = layer_norm(x, gain_ref[0:1])
        nb_ref[w] = normed_b
        normed_ref[w] = normed
        inv_ref[w] = inverse
        project(normed_b, wt_ref.at[0], wkv_ref.at[0], qkvt_ref.at[w], kv_ref.at[w])
        for group in GROUPS:
            regular_forward(
                group, qkvt_ref.at[w], kv_ref.at[w], e_ref.at[w], r_ref.at[w], o_ref.at[w]
            )
        branch = dot(pt_ref[...], o_ref[w].astype(BF16)).T
        middle.stage(w, (x + branch).astype(BF16).reshape(WIN, 64, C))

        @pl.when(w == 0)
        def _():
            wait_for_peers()
            loop(0, 4, cot.start)

        middle.start(w)

    loop(0, 4, regular_window)

    loop(0, 4, cot.arrived)
    cot.edge_arrived()
    middle.arrived(0)

    def shifted_window(w):
        @pl.when(w < 3)
        def _():
            middle.arrived(w + 1)

        @pl.when(w == 3)
        def _():
            middle.edge_arrived()

        x = halves(middle.grid[w + 1].reshape(TOK, C), middle.grid[w].reshape(TOK, C))
        normed_b, normed, inverse = layer_norm(x, gain_ref[1:2])
        project(normed_b, wt_ref.at[1], wkv_ref.at[1], qkvt1_ref, kv1_ref)
        g = halves(cot.grid[w + 1].reshape(TOK, C), cot.grid[w].reshape(TOK, C))
        g_b = g.astype(BF16)
        da_ref[0] = dot_t(p_ref[1], g_b)
        bias = bias_ref[w // 3]
        for group in GROUPS:
            shifted_both(group, qkvt1_ref, kv1_ref, bias, o1_ref, da_ref.at[0], dqkvt_ref.at[0])
        add_projection(total_ref.at[1], o1_ref[...], g_b)
        sums = dot(dqkvt_ref[0], normed_b)
        total_ref[1, :FIRST] += sums[:FIRST]
        total_ref[1, 512:704] += sums[FIRST:]
        d_normed = dot(wp_ref[1], dqkvt_ref[0]).T
        grad = g + norm_back(d_normed, normed, inverse, gain_ref[1:2])
        back.stage(w, grad.astype(BF16).reshape(WIN, 64, C))
        back.start(w)

    loop(0, 4, shifted_window)
    sum1.start()
    back.arrived(0)

    def first_heads(t):
        w = lax.rem(t + 1, 4)

        @pl.when(t < 3)
        def _():
            back.arrived(t + 1)

        @pl.when(t == 3)
        def _():
            back.edge_arrived()

        @pl.when(t == 3)
        def _():
            sum1.middle()

        g = halves(back.grid[w].reshape(TOK, C), back.grid[w + 1].reshape(TOK, C))
        g_b = g.astype(BF16)
        gb_ref[w] = g_b
        da_ref[w] = dot_t(p_ref[0], g_b)
        for group in ((0, 1), (2, 3)):
            regular_backward(
                group, qkvt_ref.at[w], kv_ref.at[w], e_ref.at[w], r_ref.at[w], o_ref.at[w],
                da_ref.at[w], dqkvt_ref.at[w],
            )
        add_projection(total_ref.at[0], o_ref[w].astype(BF16), g_b)
        total_ref[0, :FIRST] += dot(dqkvt_ref[w, :FIRST], nb_ref[w])

    loop(0, 4, first_heads)
    suma.start()

    def last_heads(w):
        @pl.when(w == 2)
        def _():
            sum1.spread(factor)

        regular_backward(
            (4, 5), qkvt_ref.at[w], kv_ref.at[w], e_ref.at[w], r_ref.at[w], o_ref.at[w],
            da_ref.at[w], dqkvt_ref.at[w],
        )
        total_ref[0, 512:704] += dot(dqkvt_ref[w, FIRST:], nb_ref[w])

    loop(0, 4, last_heads)
    sumb.start()

    def result(w):
        return pltpu.make_async_copy(
            x32_ref.at[:, :, columns(w), :], out_ref.at[:, :, columns(w), :], osem.at[w]
        )

    def input_gradient(w):
        @pl.when(w == 2)
        def _():
            suma.middle()

        d_normed = dot(wp_ref[0], dqkvt_ref[w]).T
        out = gb_ref[w].astype(F32) + norm_back(d_normed, normed_ref[w], inv_ref[w], gain_ref[0:1])
        x32_ref[:, :, columns(w), :] = out.reshape(WIN, WIN, WIN, C)
        result(w).start()

    loop(0, 4, input_gradient)
    sumb.middle()
    suma.spread(factor)
    for halo in (cot, middle, back):
        halo.finish()
    sum1.finish(res1_ref)
    sum1.drain()
    sumb.spread(factor)
    loop(0, 4, lambda w: result(w).wait())
    suma.finish(resa_ref)
    suma.drain()
    sumb.finish(resb_ref)
    sumb.drain()


def add_projection(total, attended_t, g_b):
    sums = dot(attended_t, g_b)
    total[FIRST:512] += sums[:128]
    total[704:768] += sums[128:]


def deliver(
    raw_ref, res1_ref, resa_ref, resb_ref, gain_ref, w_ref, out_ref, ggain_ref, gqkv_ref, gproj_ref,
    held, sem,
):
    loads = [pltpu.make_async_copy(raw_ref.at[d], held.at[d], sem.at[0, d]) for d in range(WIN)]
    copies = [pltpu.make_async_copy(held.at[d], out_ref.at[d], sem.at[1, d]) for d in range(WIN)]
    for load in loads:
        load.start()
    for load, copy in zip(loads, copies):
        load.wait()
        copy.start()
    pieces = [
        [resa_ref[...].astype(F32), resb_ref[...].astype(F32)],
        [res1_ref[slice(*p)].astype(F32) for p in PIECES],
    ]
    for block, (a, b) in enumerate(pieces):
        order = (a[:128], b[:64], a[128:256], b[64:128], a[256:FIRST], b[128:C])
        sums = jnp.concatenate(order, axis=0).T
        gqkv_ref[block] = sums
        gproj_ref[block] = jnp.concatenate([a[FIRST:], b[C:]], axis=0)
        gain = jnp.sum((w_ref[block].astype(F32) * sums).T, axis=0, keepdims=True)
        ggain_ref[block : block + 1] = gain / gain_ref[block : block + 1]
    for copy in copies:
        copy.wait()


def local(tokens, cotangent, gains, qkv_weight, proj_weight):
    depth_count, row_count, col_count, features = tokens.shape
    ny, nx = lax.axis_size("gy"), lax.axis_size("gx")
    factor = (depth_count * row_count * col_count * ny * nx // 16) ** (-0.5)
    whole = pl.BlockSpec(memory_space=pltpu.VMEM)
    anywhere = pl.BlockSpec(memory_space=pl.ANY)
    grad_shape = jax.ShapeDtypeStruct((WIN, WIN, 32, C), F32)
    counts = (768, 512, 256)
    nxx, nlow, nz = sizes_of(ny, nx)
    n1, n2 = nxx * nz, 4 * nlow
    scratch = [
        ((WIN, WIN, 32, C), F32),
        ((2, 3 * C, C), BF16),
        ((2, C, 3 * C), BF16),
        ((2, C, 2 * C), BF16),
        ((C, C), BF16),
        ((2, HALF, HALF), F32),
        ((4, HEADS, TOK, TOK), BF16),
        ((4, 8, TOK), F32),
        ((4, C, TOK), F32),
        ((4, 3 * C, TOK), BF16),
        ((4, TOK, 2 * C), BF16),
        ((4, TOK, C), BF16),
        ((4, TOK, C), F32),
        ((4, TOK, 1), F32),
        ((3 * C, TOK), BF16),
        ((TOK, 2 * C), BF16),
        ((C, TOK), BF16),
        ((4, C, TOK), F32),
        ((4, 3 * C, TOK), BF16),
        ((4, TOK, C), BF16),
        ((2, 4 * C, C), F32),
        ((3, 4, WIN, 64, C), BF16),
        ((3, 5, WIN, 64, C), BF16),
        ((3, WIN, 32, C), BF16),
        ((3, WIN, 32, C), BF16),
    ]
    for count in counts:
        size = count // n1
        scratch += [((k, size, C), BF16) for k in (n1, n1, n2, n1)]
    sems = [(3, 6), (3, 6), (3, n1), (3, n1), (3, n2), (3, n2), (3, n1), (3, n1), (4,)]
    raw, res1, resa, resb = pl.pallas_call(
        functools.partial(kernel, factor),
        out_shape=[grad_shape] + [jax.ShapeDtypeStruct((count, C), BF16) for count in counts],
        in_specs=[whole] * 5,
        out_specs=[anywhere] + [whole] * 3,
        scratch_shapes=[pltpu.VMEM(*s) for s in scratch]
        + [pltpu.SemaphoreType.DMA(s) for s in sems],
        compiler_params=pltpu.CompilerParams(
            vmem_limit_bytes=60 * 2**20, collective_id=0, has_side_effects=True
        ),
    )(tokens, cotangent, gains, qkv_weight, proj_weight)
    outs = [((2, C), F32), ((2, C, 3 * C), F32), ((2, C, C), F32)]
    return pl.pallas_call(
        deliver,
        out_shape=[grad_shape] + [jax.ShapeDtypeStruct(*o) for o in outs],
        in_specs=[anywhere] + [whole] * 5,
        out_specs=[anywhere] + [whole] * 3,
        scratch_shapes=[
            pltpu.VMEM((WIN, WIN, 32, C), F32),
            pltpu.SemaphoreType.DMA((2, WIN)),
        ],
        compiler_params=pltpu.CompilerParams(vmem_limit_bytes=60 * 2**20),
    )(raw, res1, resa, resb, gains, qkv_weight)


def solution(mesh):
    in_specs = (P(None, "gy", "gx", None), P(None, "gy", "gx", None), P(), P(), P())
    out_specs = (P(None, "gy", "gx", None), P(), P(), P())
    return jax.shard_map(local, mesh=mesh, in_specs=in_specs, out_specs=out_specs, check_vma=False)
```

time: 93.6 us -> 80.6 us (0.86)
  Pallas kernels: 87.2 us -> 79.6 us
  local copies, waits for them, and re-layouts: 5.54 us -> 0 us
    pallas_call x1 -> x2, Pallas kernels: 87.2 us -> 79.6 us  [the longest x1 74.9 us: local(): pl.pallas_call(functools.partial(kernel, factor), out_shape=[grad_shape]...]
    unnamed x10 -> x0, local copies, waits for them, and re-layouts: 5.54 us -> none
where the time goes in v3:
time: 80.6 us; the launch traced here: 80.3 us
  Pallas kernels  79.6 us (99%)
    pallas_call x1, Pallas kernels, local(): pl.pallas_call(functools.partial(kernel, factor), out_shape=[grad_shape]...  74.9 us
    pallas_call x1, Pallas kernels, local(): pl.pallas_call(deliver, out_shape=[grad_shape] + [jax.ShapeDtypeStruct(*o...  4.76 us

profile of v3, /device:TPU:1, one launch (start us, length us, event | category | flops | bytes accessed | tf_op | source)
XLA Modules:
  0.0 80.3 jit_solution(4358000261621121520)
XLA Ops:
  0.6 74.9 %shard_map.84 = (f32[8,8,32,192]{3,2,1,0:T(8,128)}, bf16[768,192]{1,0:T(8,128)(2,1)}, bf16[512,192]{1,0:T(8,128)(2,1)}, bf16[256,192]{1,0:T(8,128)(2,1)}) custom-call(bf16[8,8,32,192]{3,2,1,0:T(8,128)(2,1)} %tok_ref.1, bf16[8,8,32,192]{3,2,1,0:T(8,128)(2,1)} %cot_ref.1, f32[2,192]{1,0:T(2,128)} %gain_ref.3, bf16[2,192,576]{2,1,0:T(8,128)(2,1)} %w_ref.3, ...), custom_call_target="tpu_custom_call" | custom-call | tf_op jit(solution)/shard_map/pallas_call | solution.py:612
  75.5 4.8 %shard_map.85 = (f32[8,8,32,192]{3,2,1,0:T(8,128)}, f32[2,192]{1,0:T(2,128)}, f32[2,192,576]{2,1,0:T(8,128)}, f32[2,192,192]{2,1,0:T(8,128)}) custom-call(f32[8,8,32,192]{3,2,1,0:T(8,128)} %get-tuple-element.8.raw_ref, bf16[768,192]{1,0:T(8,128)(2,1)} %get-tuple-element.9.res1_ref, bf16[512,192]{1,0:T(8,128)(2,1)} %get-tuple-element.10.resa_ref, ...), custom_call_target="tpu_custom_call" | custom-call | tf_op jit(solution)/shard_map/pallas_call | solution.py:624
